TPU v7x, 256 devices: a whole 4x4x8 slice. The times are simulated.
256 devices in a mesh: section: 2 (over x_hi), dp: 128 (over x_lo, z, y, core).
Axes of the slice: x: 4 (x_hi: 2, x_lo: 2; x = x_hi * 2 + x_lo), y: 4, z: 8, core: 2. Of those that a mesh axis runs over, the one named last changes fastest.
Arguments:
- heat_start: float32 [4096, 32, 128], P(('section', 'dp')), may hold values from -18 to 18
- conductivity: float32 [4096, 32, 128], P(('section', 'dp')), may hold values from 0.25 to 1
- patch_z: int32 [256], P(('section', 'dp')), may hold values from 0 to 12
- patch_x: int32 [256], P(('section', 'dp')), may hold values from 0 to 24
- slot_table: int32 [256], P(('section', 'dp')), may hold values from 0 to 255, as said below
- w_stem: bfloat16 [64, 54], replicated, may hold values from -0.875 to 0.875
- w_lift: bfloat16 [64, 64], replicated, may hold values from -0.75 to 0.75
- w_down: bfloat16 [128, 1728], replicated, may hold values from -1 to 1
- w_deep: bfloat16 [128, 128], replicated, may hold values from -1 to 2
- w_merge: bfloat16 [64, 192], replicated, may hold values from -1 to 1
- w_out: bfloat16 [1, 64], replicated, may hold values from -0.75 to 0.75
Outputs:
- heat_two: float32 [4096, 32, 128], P(('section', 'dp'))
- predictions: bfloat16 [512, 4, 8, 128], P(('section', 'dp'))
- grad_pack: float32 [2048, 128], P('dp')
Inputs may be any that keep to these rules, and one draw needn't show every extreme that they name: Within each section (each aligned block of 128 entries) the entries are distinct; entry s sends patch s to trainer slot_table[s] // 2 of the same section, slot slot_table[s] % 2. In each section a quarter of the trainers receive two patches, half receive one, a quarter none.
All inputs are finite; a program needn't handle non-finite values.
Results may differ from a plain program's by a relative error of at most 0.0073.
The roundings to bfloat16 on the way count: a program that leaves them out, or rounds other values in their place, can miss the bound.
Values may be sent and summed in bfloat16 or wider, within the bound.
A program may use at most 128 MiB of HBM per device.

v0:
```python
from functools import partial

import jax
import jax.numpy as jnp
from jax import lax
from jax.sharding import PartitionSpec as P

GY = 128
PZ = 4
PX = 8
GROWS = 2048


TIME_STEP = 0.15


def with_halo(x, sides, width):
    for axis, dim in sides:
        size, length = (lax.axis_size(axis), x.shape[dim])
        up = [(i, (i + 1) % size) for i in range(size - 1)]
        down = [(j, i) for i, j in up]
        last = lax.slice_in_dim(x, length - width, length, axis=dim)
        leading = lax.slice_in_dim(x, 0, width, axis=dim)
        before = lax.ppermute(last, axis, up)
        after = lax.ppermute(leading, axis, down)
        x = jnp.concatenate([before, x, after], axis=dim)
    return x


def advance(heat_ext, cond_ext):
    interior = heat_ext[1:-1]
    cond_mid = cond_ext[1:-1]
    padded_u = jnp.pad(interior, ((0, 0), (1, 1), (1, 1)))
    padded_k = jnp.pad(cond_mid, ((0, 0), (1, 1), (1, 1)))
    net_flux = 0.5 * (cond_mid + cond_ext[2:]) * (heat_ext[2:] - interior)
    net_flux = net_flux + 0.5 * (cond_mid + cond_ext[:-2]) * (heat_ext[:-2] - interior)
    net_flux = net_flux + 0.5 * (cond_mid + padded_k[:, 2:, 1:-1]) * (
        padded_u[:, 2:, 1:-1] - interior
    )
    net_flux = net_flux + 0.5 * (cond_mid + padded_k[:, :-2, 1:-1]) * (
        padded_u[:, :-2, 1:-1] - interior
    )
    net_flux = net_flux + 0.5 * (cond_mid + padded_k[:, 1:-1, 2:]) * (
        padded_u[:, 1:-1, 2:] - interior
    )
    net_flux = net_flux + 0.5 * (cond_mid + padded_k[:, 1:-1, :-2]) * (
        padded_u[:, 1:-1, :-2] - interior
    )
    return interior + TIME_STEP * net_flux


def conv_cube(activity, kernel):
    depth_z, width_x, width_y = (activity.shape[2], activity.shape[3], activity.shape[4])
    padded = jnp.pad(activity, ((0, 0), (0, 0), (1, 1), (1, 1), (1, 1)))
    shifted = [
        padded[
            :,
            :,
            offset_z : offset_z + depth_z,
            offset_x : offset_x + width_x,
            offset_y : offset_y + width_y,
        ]
        for offset_z in range(3)
        for offset_x in range(3)
        for offset_y in range(3)
    ]
    columns = jnp.concatenate(shifted, axis=0)
    result = jnp.dot(
        kernel, columns.reshape(columns.shape[0], -1), preferred_element_type=jnp.float32
    )
    return result.reshape((kernel.shape[0],) + activity.shape[1:])


def pointwise(kernel, activity):
    result = jnp.dot(
        kernel, activity.reshape(activity.shape[0], -1), preferred_element_type=jnp.float32
    )
    return result.reshape((kernel.shape[0],) + activity.shape[1:])


def network_loss(weights, batch_data, loss_scale):
    w_stem, w_lift, w_down, w_deep, w_merge, w_out = weights
    inputs = jnp.transpose(batch_data[:, :2], (1, 0, 2, 3, 4))
    target = batch_data[:, 2].astype(jnp.float32)
    level_one = jax.nn.silu(conv_cube(inputs, w_stem)).astype(jnp.bfloat16)
    level_two = jax.nn.silu(pointwise(w_lift, level_one)).astype(jnp.bfloat16)
    channels, batch_size, depth_z, width_x, width_y = level_two.shape
    stored = lax.optimization_barrier(level_two).astype(jnp.float32)
    pooled = (
        stored.reshape(channels, batch_size, depth_z // 2, 2, width_x // 2, 2, width_y)
        .mean(axis=(3, 5))
        .astype(jnp.bfloat16)
    )
    coarse = jax.nn.silu(conv_cube(pooled, w_down)).astype(jnp.bfloat16)
    deeper = jax.nn.silu(pointwise(w_deep, coarse)).astype(jnp.bfloat16)
    lifted = jnp.repeat(jnp.repeat(deeper, 2, axis=2), 2, axis=3)
    joined = jnp.concatenate([level_two, lifted], axis=0)
    merged = jax.nn.silu(pointwise(w_merge, joined)).astype(jnp.bfloat16)
    predicted = pointwise(w_out, merged)[0]
    misfit = predicted - target
    loss_value = 0.5 * jnp.sum(misfit * misfit) * loss_scale
    return (loss_value, predicted)


def train_slots(weights, batch_data, loss_scale):
    loss_value, pullback, predicted = jax.vjp(
        partial(network_loss, batch_data=batch_data, loss_scale=loss_scale), weights, has_aux=True
    )
    gradients = pullback(jnp.ones((), jnp.float32))[0]
    return (gradients, predicted)


def pack_grads(gradients, row_count):
    flattened = jnp.concatenate(
        [grad_piece.astype(jnp.float32).reshape(-1) for grad_piece in gradients]
    )
    flattened = jnp.pad(flattened, (0, row_count * 128 - flattened.shape[0]))
    return flattened.reshape(row_count, 128)


def local(
    heat_start,
    conductivity,
    patch_z,
    patch_x,
    slot_table,
    w_stem,
    w_lift,
    w_down,
    w_deep,
    w_merge,
    w_out,
):
    weights = (w_stem, w_lift, w_down, w_deep, w_merge, w_out)
    paired = jnp.stack([heat_start, conductivity])
    widened = with_halo(paired, ((("section", "dp"), 1),), 1)
    heat_one = advance(widened[0], widened[1])
    heat_ext = with_halo(heat_one.astype(jnp.bfloat16), ((("section", "dp"), 0),), 1).astype(
        heat_one.dtype
    )
    heat_two = advance(heat_ext, widened[1])
    stacked = jnp.stack([heat_one, conductivity, heat_two])
    zero_index = jnp.zeros((), jnp.int32)
    own_patch = lax.dynamic_slice(
        stacked, (zero_index, patch_z[0], patch_x[0], zero_index), (3, PZ, PX, GY)
    ).astype(jnp.bfloat16)
    peer_count = lax.axis_size("dp")
    dp_index = lax.axis_index("dp")
    table_all = lax.all_gather(slot_table, "dp", axis=0, tiled=True)
    receivers = jnp.arange(2, dtype=jnp.int32)[:, None] + 2 * dp_index
    picker = (table_all[None, :] == receivers).astype(jnp.bfloat16)
    sender_mask = (jnp.arange(peer_count, dtype=jnp.int32) == slot_table[0] // 2).astype(
        jnp.bfloat16
    )[:, None]
    loss_scale = 1.0 / (lax.axis_size("section") * peer_count * PZ * PX * GY)
    outgoing = sender_mask * own_patch.reshape(1, -1)
    incoming = lax.all_to_all(outgoing, "dp", split_axis=0, concat_axis=0, tiled=True)
    slot_data = jnp.dot(picker, incoming, preferred_element_type=jnp.float32).astype(jnp.bfloat16)
    gradients, predicted = train_slots(weights, slot_data.reshape(2, 3, PZ, PX, GY), loss_scale)
    predictions = predicted.astype(jnp.bfloat16)
    packed = pack_grads(gradients, GROWS)
    grad_shard = lax.psum_scatter(packed, "dp", scatter_dimension=0, tiled=True)
    summed = lax.psum(grad_shard, "section")
    return (heat_two, predictions, summed)


def solution(mesh):
    return jax.shard_map(
        local,
        mesh=mesh,
        in_specs=(
            P(("section", "dp"), None, None),
            P(("section", "dp"), None, None),
            P(("section", "dp")),
            P(("section", "dp")),
            P(("section", "dp")),
            P(),
            P(),
            P(),
            P(),
            P(),
            P(),
        ),
        out_specs=(
            P(("section", "dp"), None, None),
            P(("section", "dp"), None, None, None),
            P("dp", None),
        ),
        check_vma=False,
    )
```

profile of v0, /device:TPU:1, one launch (start us, length us, event | category | flops | bytes accessed | tf_op | source)
XLA Modules:
  0.0 1015.6 jit_solution(14494389145235105602)
XLA Ops:
  8.1 5.1 collective-permute-start
  16.3 3.4 fusion.130
  19.8 4.1 collective-permute-start.2
  30.0 6.7 broadcast_multiply_fusion
  37.1 20.6 %reduce = bf16[128,12288]{1,0:T(8,128)(2,1)} reduce(bf16[128,1,12288]{2,1,0:T(2,128)(2,1)} %broadcast_multiply_fusion, bf16[]{:T(256)} %broadcast.186), dimensions={1}, to_apply=%broadcast_multiply_fusion.reduce_sub_computation | reduce | bytes 6291458 | tf_op jit(solution)/shard_map/mul | solution.py:156
  57.8 8.1 reshape.275
  65.8 24.5 %all-to-all-start = ((bf16[128,2,6144]{2,1,0:T(2,128)(2,1)}), bf16[128,2,6144]{2,1,0:T(2,128)(2,1)}, u32[]{:S(2)}, u32[]{:S(2)}) async-start(bf16[128,2,6144]{2,1,0:T(2,128)(2,1)} %reshape.275), calls=%async_computation | async-start | bytes 6291456 | tf_op jit(solution)/shard_map/all_to_all | solution.py:157
  91.7 77.0 %all-reduce.33 = s32[128]{0:T(128)S(1)} all-reduce(s32[128]{0:T(128)S(1)} %dynamic-update-slice), channel_id=1, replica_groups=mesh['section'=2,'dp'=128] {'dp'}, use_global_device_ids=true, to_apply=%add.33 | all-reduce | flops 128 | bytes 1024
  169.2 19.5 %reshape.276 = bf16[128,1,12288]{2,1,0:T(2,128)(2,1)} reshape(bf16[128,2,6144]{2,1,0:T(2,128)(2,1)} %all-to-all-done) | data formatting | bytes 6291456
  188.8 6.2 fusion.72
  225.8 10.0 copy.231
  235.8 6.1 fusion.110
  250.9 2.7 copy.235
  268.8 4.8 reshape.239
  273.6 8.1 reduce_sum.28
  281.7 2.9 reduce_sum.29
  304.6 3.0 fusion.67
  307.7 2.6 copy.275
  312.9 6.5 fusion.15
  417.5 6.0 pad_add_fusion
  433.1 2.9 fusion.79
  436.9 4.1 dynamic-update-slice.3
  444.0 557.1 %reduce-scatter.2.cloned.1.call-done = f32[16,128]{1,0:T(8,128)} async-done(((f32[2048,128]{1,0:T(8,128)}), f32[16,128]{1,0:T(8,128)}) %reduce-scatter.2.cloned.1.call-update) | async-done | bytes 8208 | tf_op jit(solution)/shard_map/reduce_scatter | solution.py:162
  1001.1 7.2 psum.7
  (252 shorter events, 199.1 us)
Async XLA Ops:
  7.2 228.6 %copy-start = (bf16[128,1728]{0,1:T(8,128)(2,1)S(1)}, bf16[128,1728]{0,1:T(8,128)(2,1)}, u32[]{:S(2)}) copy-start(bf16[128,1728]{0,1:T(8,128)(2,1)} %param.18) | copy-start | bytes 1327108
  7.2 21.7 %copy-start.3 = (f32[16,32,128]{2,1,0:T(8,128)S(1)}, f32[16,32,128]{2,1,0:T(8,128)}, u32[]{:S(2)}) copy-start(f32[16,32,128]{2,1,0:T(8,128)} %param.12) | copy-start | bytes 786436
  7.2 21.7 %copy-start.12 = (f32[16,32,128]{2,1,0:T(8,128)S(1)}, f32[16,32,128]{2,1,0:T(8,128)}, u32[]{:S(2)}) copy-start(f32[16,32,128]{2,1,0:T(8,128)} %param.11) | copy-start | bytes 786436
  8.1 7.7 collective-permute-start
  13.2 3.1 collective-permute-start.1
  19.8 7.3 collective-permute-start.2
  23.8 5.0 collective-permute-start.3
  65.8 24.6 %copy-start.40 = (u32[256]{0:T(256)S(1)}, u32[256]{0:T(256)}, u32[]{:S(2)}) copy-start(u32[256]{0:T(256)} %constant.124) | copy-start | bytes 3076
  65.8 102.9 %copy-start.37 = (bf16[1,64]{1,0:T(2,128)(2,1)S(1)}, bf16[1,64]{1,0:T(2,128)(2,1)}, u32[]{:S(2)}) copy-start(bf16[1,64]{1,0:T(2,128)(2,1)} %param.21) | copy-start | bytes 388
  65.8 103.4 %all-to-all-start = ((bf16[128,2,6144]{2,1,0:T(2,128)(2,1)}), bf16[128,2,6144]{2,1,0:T(2,128)(2,1)}, u32[]{:S(2)}, u32[]{:S(2)}) async-start(bf16[128,2,6144]{2,1,0:T(2,128)(2,1)} %reshape.275), calls=%async_computation | async-start | bytes 6291456 | tf_op jit(solution)/shard_map/all_to_all | solution.py:157
  90.3 910.8 %reduce-scatter.2.cloned.1.call-start = ((), (), s32[]{:S(2)}) async-start(), calls=%async_computation.2 | async-start | bytes 1056768 | tf_op jit(solution)/shard_map/reduce_scatter | solution.py:162
  203.4 3.5 copy-start.8
  235.8 6.9 copy-start.31
  262.2 3.4 copy-start.17
  262.2 3.4 copy-start.22
  296.9 3.8 copy-start.23
  417.4 6.1 copy-start.25
  417.5 6.1 copy-start.26
  417.5 6.1 copy-start.27
  417.5 6.1 copy-start.28
  417.5 6.1 copy-start.29
  433.1 3.8 copy-start.21
  433.1 8.0 copy-start.32
  433.1 575.2 %copy-start.1 = (bf16[128,1728]{0,1:T(8,128)(2,1)S(1)}, bf16[128,1728]{0,1:T(8,128)(2,1)}, u32[]{:S(2)}) copy-start(bf16[128,1728]{0,1:T(8,128)(2,1)} %param.18) | copy-start | bytes 1327108
  (23 other events, 43.1 us)
Sparse Core Ops, SparseCore 0:
  443.5 557.5 reduce-scatter.1
where the time goes:
time: 1030 us; the launch traced here: 1020 us
  waiting for transfers between devices  559 us (54%)
  local copies, waits for them, and re-layouts  214 us (21%)
  blocking collectives  84.2 us (8%)
  other arithmetic  64.5 us (6%)
  matrix products  38.5 us (4%)
  starting transfers between devices  37.5 us (4%)
  between operations  17.2 us (2%)
    reduce_scatter x1, waiting for transfers between devices, local(): grad_shard = lax.psum_scatter(packed, 'dp', scatter_dimension=0, tiled=True)  557 us
    split x56, local copies, waits for them, and re-layouts, conv_cube(): columns = jnp.concatenate(shifted, axis=0)  97.2 us
    unnamed x1, blocking collectives  77 us
    unnamed x129, local copies, waits for them, and re-layouts  70.5 us
    mul x2, other arithmetic, local(): outgoing = sender_mask * own_patch.reshape(1, -1)  27.3 us
    all_to_all x1, starting transfers between devices, local(): lax.all_to_all(outgoing, 'dp', split_axis=0, concat_axis=0, tiled=True)  24.5 us
  transfers between devices with their start and end apart: 6, of which 3 were waited for; matrix products, arithmetic and copies ran while one was open for 0% of the time, Pallas kernels for 0%

commit v1 on v0

v1 whole, which is shorter than its diff:
```python
import functools

import jax
import jax.numpy as jnp
from jax import lax
from jax.experimental import pallas as pl
from jax.experimental.pallas import tpu as pltpu
from jax.sharding import PartitionSpec as P

MESH = pl.DeviceIdType.MESH
TIME_STEP = 0.15
GY = 128
PZ = 4
PX = 8
C1 = 64
C2 = 128
GROWS = 2048
LINE = 8
F32 = jnp.float32
BF16 = jnp.bfloat16
VMEM = pl.BlockSpec(memory_space=pltpu.VMEM)
SMEM = pl.BlockSpec(memory_space=pltpu.SMEM)


def rounded(x):
    return x.astype(BF16).astype(F32)


def heat_kernel(
    n_sec, n_dp, pz_ref, px_ref, u_ref, k_ref, out_ref, patch_ref, ulo, klo, uhi, khi, h1, send, recv
):
    total = n_sec * n_dp
    depth = u_ref.shape[0]
    me = lax.axis_index("section") * n_dp + lax.axis_index("dp")
    after = lax.rem(me + 1, total)
    before = lax.rem(me + total - 1, total)

    def place(i):
        return (lax.div(i, n_dp), lax.rem(i, n_dp))

    barrier = pltpu.get_barrier_semaphore()
    for peer in (before, after):
        pl.semaphore_signal(barrier, inc=1, device_id=place(peer), device_id_type=MESH)
    pl.semaphore_wait(barrier, 2)
    plan = (
        (u_ref.at[pl.ds(depth - 2, 2)], ulo, after),
        (k_ref.at[pl.ds(depth - 2, 2)], klo, after),
        (u_ref.at[pl.ds(0, 2)], uhi, before),
        (k_ref.at[pl.ds(0, 2)], khi, before),
    )
    copies = []
    for i, (src, dst, peer) in enumerate(plan):
        copy = pltpu.make_async_remote_copy(
            src_ref=src,
            dst_ref=dst,
            send_sem=send.at[i],
            recv_sem=recv.at[i],
            device_id=place(peer),
            device_id_type=MESH,
        )
        copy.start()
        copies.append(copy)

    rows, lanes = u_ref.shape[1:]
    row = lax.broadcasted_iota(jnp.int32, (rows, lanes), 0)
    lane = lax.broadcasted_iota(jnp.int32, (rows, lanes), 1)

    def step(up, uc, un, kp, kc, kn):
        flux = (kc + kn) * (un - uc) + (kc + kp) * (up - uc)
        for axis, place_, size in ((0, row, rows), (1, lane, lanes)):
            last = place_ == size - 1
            first = place_ == 0
            u_next = jnp.where(last, 0.0, pltpu.roll(uc, size - 1, axis))
            k_next = jnp.where(last, 0.0, pltpu.roll(kc, size - 1, axis))
            face = (kc + k_next) * (u_next - uc)
            back = jnp.where(first, kc * uc, pltpu.roll(face, 1, axis))
            flux = flux + (face - back)
        return uc + (0.5 * TIME_STEP) * flux

    def interior(z, carry):
        h1[z + 1] = step(u_ref[z - 1], u_ref[z], u_ref[z + 1], k_ref[z - 1], k_ref[z], k_ref[z + 1])
        return carry

    lax.fori_loop(1, depth - 1, interior, 0)
    for copy in copies:
        copy.wait_recv()
    has_lo = (me > 0).astype(F32)
    has_hi = (me < total - 1).astype(F32)
    ul = [ulo[0] * has_lo, ulo[1] * has_lo]
    kl = [klo[0] * has_lo, klo[1] * has_lo]
    uh = [uhi[0] * has_hi, uhi[1] * has_hi]
    kh = [khi[0] * has_hi, khi[1] * has_hi]
    end = depth - 1
    h1[0] = has_lo * step(ul[0], ul[1], u_ref[0], kl[0], kl[1], k_ref[0])
    h1[1] = step(ul[1], u_ref[0], u_ref[1], kl[1], k_ref[0], k_ref[1])
    h1[depth] = step(u_ref[end - 1], u_ref[end], uh[0], k_ref[end - 1], k_ref[end], kh[0])
    h1[depth + 1] = has_hi * step(u_ref[end], uh[0], uh[1], k_ref[end], kh[0], kh[1])

    out_ref[0] = step(h1[0], h1[1], h1[2], kl[1], k_ref[0], k_ref[1])
    out_ref[end] = step(h1[end], h1[depth], h1[depth + 1], k_ref[end - 1], k_ref[end], kh[0])

    def second(z, carry):
        out_ref[z] = step(h1[z], h1[z + 1], h1[z + 2], k_ref[z - 1], k_ref[z], k_ref[z + 1])
        return carry

    lax.fori_loop(1, depth - 1, second, 0)
    pz = pz_ref[0]
    px = px_ref[0]
    for z in range(PZ):
        patch_ref[0, z] = h1[1 + pz + z, pl.ds(px, PX), :]
        patch_ref[1, z] = k_ref[pz + z, pl.ds(px, PX), :]
        patch_ref[2, z] = out_ref[pz + z, pl.ds(px, PX), :]
    for copy in copies:
        copy.wait_send()


def heat_steps(n_sec, n_dp, heat, cond, patch_z, patch_x):
    layers = (2,) + heat.shape[1:]
    return pl.pallas_call(
        functools.partial(heat_kernel, n_sec, n_dp),
        out_shape=(
            jax.ShapeDtypeStruct(heat.shape, F32),
            jax.ShapeDtypeStruct((3, PZ, PX, GY), F32),
        ),
        in_specs=[SMEM, SMEM, VMEM, VMEM],
        out_specs=(VMEM, VMEM),
        scratch_shapes=[
            pltpu.VMEM(layers, F32),
            pltpu.VMEM(layers, F32),
            pltpu.VMEM(layers, F32),
            pltpu.VMEM(layers, F32),
            pltpu.VMEM((heat.shape[0] + 2,) + heat.shape[1:], F32),
            pltpu.SemaphoreType.DMA((4,)),
            pltpu.SemaphoreType.DMA((4,)),
        ],
        compiler_params=pltpu.CompilerParams(
            collective_id=0, has_side_effects=True, vmem_limit_bytes=16 * 2**20
        ),
        name="heat",
    )(patch_z, patch_x, heat, cond)


NT = (((1,), (1,)), ((), ()))
NN = (((1,), (0,)), ((), ()))


def mm(a, b, dims=NN):
    return lax.dot_general(a, b, dims, preferred_element_type=F32)


def silu_and_slope(z):
    s = 0.5 * jnp.tanh(0.5 * z) + 0.5
    value = z * s
    return value, s + value * (1.0 - s)


def block(x, b):
    return x[:, b * GY : (b + 1) * GY]


def train_kernel(
    scale,
    slot_ref,
    patch_ref,
    w_stem,
    w_lift,
    w_down,
    w_deep,
    w_merge,
    w_out,
    pred_ref,
    grad_ref,
    tall,
    cols,
    l1,
    l2,
    g1,
    g2,
    dl2,
    colsd,
    colsz,
    wback,
    pack,
    pair,
):
    plane = PX * GY
    cells = PZ * plane
    small = cells // 4
    row8 = lax.broadcasted_iota(jnp.int32, (PX, GY), 0)
    lane8 = lax.broadcasted_iota(jnp.int32, (PX, GY), 1)
    lane64 = lax.broadcasted_iota(jnp.int32, (C1, GY), 1)

    tall[...] = jnp.zeros_like(tall)
    for channel in range(2):
        for dx in range(3):
            for dy in range(3):
                shifted = []
                for z in range(PZ):
                    v = rounded(patch_ref[channel, z])
                    if dx == 0:
                        v = jnp.where(row8 == 0, 0.0, pltpu.roll(v, 1, 0))
                    elif dx == 2:
                        v = jnp.where(row8 == PX - 1, 0.0, pltpu.roll(v, PX - 1, 0))
                    if dy == 0:
                        v = jnp.where(lane8 == 0, 0.0, pltpu.roll(v, 1, 1))
                    elif dy == 2:
                        v = jnp.where(lane8 == GY - 1, 0.0, pltpu.roll(v, GY - 1, 1))
                    shifted.append(v)
                for dz in range(3):
                    r = ((dz * 3 + dx) * 3 + dy) * 2 + channel
                    for z in range(PZ):
                        if 0 <= z + dz - 1 < PZ:
                            tall[pl.ds(z * PX * C1 + r, PX, stride=C1), :] = shifted[z + dz - 1]
    for b in range(PZ * PX):
        cols[:, b * GY : (b + 1) * GY] = tall[b * C1 : (b + 1) * C1, :].astype(BF16)

    stem = w_stem[...]
    lift = w_lift[...]
    taps = stem.shape[1]
    pooled = []
    for zz in range(PZ // 2):
        rows = []
        for z in (2 * zz, 2 * zz + 1):
            here = slice(z * plane, (z + 1) * plane)
            value, slope = silu_and_slope(mm(stem, cols[0:taps, here]))
            g1[:, here] = slope
            one = value.astype(BF16)
            l1[:, here] = one
            value, slope = silu_and_slope(mm(lift, one))
            g2[:, here] = slope
            two = value.astype(BF16)
            l2[:, here] = two
            rows.append(two.astype(F32))
        both = rows[0] + rows[1]
        for xx in range(PX // 2):
            pooled.append(rounded((block(both, 2 * xx) + block(both, 2 * xx + 1)) * 0.25))

    hz, hx = PZ // 2, PX // 2
    shifted = []
    for dy in range(3):
        if dy == 0:
            part = [jnp.where(lane64 == 0, 0.0, pltpu.roll(v, 1, 1)) for v in pooled]
        elif dy == 1:
            part = pooled
        else:
            part = [jnp.where(lane64 == GY - 1, 0.0, pltpu.roll(v, GY - 1, 1)) for v in pooled]
        shifted.append([v.astype(BF16) for v in part])
    nothing = jnp.zeros((C1, GY), BF16)
    for dz in range(3):
        for dx in range(3):
            for dy in range(3):
                r = ((dz * 3 + dx) * 3 + dy) * C1
                for z in range(hz):
                    for x in range(hx):
                        sz, sx = z + dz - 1, x + dx - 1
                        inside = 0 <= sz < hz and 0 <= sx < hx
                        b = z * hx + x
                        colsd[r : r + C1, b * GY : (b + 1) * GY] = (
                            shifted[dy][sz * hx + sx] if inside else nothing
                        )
    depth = 27 * C1
    colsd[depth : depth + C1, :] = jnp.zeros((C1, small), BF16)
    value, slope_down = silu_and_slope(mm(w_down[...], colsd[0:depth, :]))
    coarse = value.astype(BF16)
    value, slope_deep = silu_and_slope(mm(w_deep[...], coarse))
    deeper = value.astype(BF16)
    merge_fine = w_merge[:, 0:C1]
    merge_coarse = w_merge[:, C1 : C1 + C2]
    lifted = mm(merge_coarse, deeper)

    out_row = w_out[...].astype(F32)
    eye = lax.broadcasted_iota(jnp.int32, (C1, C1), 0) == lax.broadcasted_iota(jnp.int32, (C1, C1), 1)
    out_col = jnp.sum(jnp.where(eye, jnp.broadcast_to(out_row, (C1, C1)), 0.0), axis=1, keepdims=True)
    out8 = jnp.broadcast_to(out_row, (8, C1)).astype(BF16)
    fine_t = merge_fine.astype(F32).T.astype(BF16)
    d_fine = jnp.zeros((C1, GY), F32)
    d_out = jnp.zeros((8, GY), F32)
    gathered = [None] * (hz * hx)
    for z in range(PZ):
        here = slice(z * plane, (z + 1) * plane)
        two = l2[:, here]
        added = [block(lifted, (z // 2) * hx + x // 2) for x in range(PX)]
        value, slope = silu_and_slope(mm(merge_fine, two) + jnp.concatenate(added, axis=1))
        merged = value.astype(BF16)
        wide = mm(out8, merged)
        predicted = jnp.zeros((PX, GY), F32)
        for x in range(PX):
            predicted = jnp.where(row8 == x, block(wide, x), predicted)
        pred_ref[z * PX : (z + 1) * PX, :] = predicted
        misfit = (predicted - rounded(patch_ref[2, z])) * scale
        d_wide = jnp.concatenate(
            [jnp.broadcast_to(misfit[x : x + 1, :], (8, GY)) for x in range(PX)], axis=1
        ).astype(BF16)
        d_out = d_out + mm(d_wide, jnp.concatenate([merged, merged], axis=0), NT)
        d_merged = jnp.concatenate([out_col * misfit[x : x + 1, :] for x in range(PX)], axis=1)
        dz = rounded(d_merged) * slope
        for x in range(PX):
            b = (z // 2) * hx + x // 2
            gathered[b] = block(dz, x) if gathered[b] is None else gathered[b] + block(dz, x)
        dz = dz.astype(BF16)
        d_fine = d_fine + mm(dz, jnp.concatenate([two, two], axis=0), NT)
        dl2[:, here] = rounded(mm(fine_t, dz))

    d_lifted = jnp.concatenate(gathered, axis=1).astype(BF16)
    d_coarse_merge = mm(d_lifted, deeper, NT)
    d_deeper = mm(merge_coarse.astype(F32).T.astype(BF16), d_lifted)
    dz_deep = (rounded(d_deeper) * slope_deep).astype(BF16)
    d_deep = mm(dz_deep, coarse, NT)
    d_coarse = mm(w_deep[...].astype(F32).T.astype(BF16), dz_deep)
    dz_down = (rounded(d_coarse) * slope_down).astype(BF16)

    r_ = lax.broadcasted_iota(jnp.int32, (C2, C2), 0)
    c_ = lax.broadcasted_iota(jnp.int32, (C2, C2), 1)
    parted = jnp.where(r_ < C1, 2 * r_, 2 * r_ - (C2 - 1)) == c_
    dz_parted = mm(parted.astype(BF16), dz_down).astype(BF16)
    base = 27 + 32
    chunks = [mm(dz_parted, colsd[j * C2 : (j + 1) * C2, :], NT) for j in range(14)]
    low = lane64 < C1
    for j in range(13):
        pack[pl.ds(base + j, C1, stride=27), :] = chunks[j][0:C1]
        pack[pl.ds(base + 14 + j, C1, stride=27), :] = pltpu.roll(
            jnp.where(low, chunks[j + 1][C1:C2], chunks[j][C1:C2]), C1, 1
        )
    pack[pl.ds(base + 13, C1, stride=27), :] = jnp.where(
        low, chunks[13][0:C1], pltpu.roll(chunks[0][C1:C2], C1, 1)
    )

    blank = jnp.zeros((C2, GY), BF16)
    for dz in range(3):
        for dx in range(3):
            j = dz * 3 + dx
            wback[:, j * C2 : (j + 1) * C2] = (
                w_down[:, j * 3 * C1 : (j + 1) * 3 * C1].astype(F32).T.astype(BF16)
            )
            for z in range(hz):
                for x in range(hx):
                    sz, sx = z - (dz - 1), x - (dx - 1)
                    inside = 0 <= sz < hz and 0 <= sx < hx
                    b = z * hx + x
                    colsz[j * C2 : (j + 1) * C2, b * GY : (b + 1) * GY] = (
                        block(dz_down, sz * hx + sx) if inside else blank
                    )
    d_shifted = mm(wback[...], colsz[...])
    d_pooled = []
    for b in range(hz * hx):
        whole = block(d_shifted, b)
        total = whole[C1 : 2 * C1]
        total = total + jnp.where(lane64 == GY - 1, 0.0, pltpu.roll(whole[0:C1], GY - 1, 1))
        total = total + jnp.where(lane64 == 0, 0.0, pltpu.roll(whole[2 * C1 : 3 * C1], 1, 1))
        d_pooled.append(rounded(total) * 0.25)

    lift_t = lift.astype(F32).T.astype(BF16)
    d_lift = jnp.zeros((C1, GY), F32)
    d_stem = jnp.zeros((C1, C1), F32)
    for z in range(PZ):
        here = slice(z * plane, (z + 1) * plane)
        spread = jnp.concatenate([d_pooled[(z // 2) * hx + x // 2] for x in range(PX)], axis=1)
        dz = ((dl2[:, here] + spread) * g2[:, here]).astype(BF16)
        one = l1[:, here]
        d_lift = d_lift + mm(dz, jnp.concatenate([one, one], axis=0), NT)
        d_one = rounded(mm(lift_t, dz))
        dz = (d_one * g1[:, here]).astype(BF16)
        d_stem = d_stem + mm(dz, cols[:, here], NT)

    pair[:, 0:C1] = d_stem
    pair[:, C1:GY] = jnp.zeros((C1, GY - C1), F32)
    turned = pair[...]
    source = lax.broadcasted_iota(jnp.int32, (C1, GY), 0)
    for bit in range(6):
        moved = pltpu.roll(turned, (taps << bit) % GY, 1)
        turned = jnp.where((source >> bit) % 2 == 1, moved, turned)
    begin = source * taps
    kept = turned.astype(BF16)
    wraps = lane64 < begin % GY
    stay = jnp.where(wraps, 0.0, turned).astype(BF16)
    over = jnp.where(wraps, turned, 0.0).astype(BF16)
    target_row = lax.broadcasted_iota(jnp.int32, (32, C1), 0)
    owner = lax.broadcasted_iota(jnp.int32, (32, C1), 1) * taps // GY
    del kept
    stem_rows = mm((target_row == owner).astype(BF16), stay)
    stem_rows = stem_rows + mm((target_row == owner + 1).astype(BF16), over)
    pack[0:27, :] = stem_rows[0:27, :]

    low32 = lax.broadcasted_iota(jnp.int32, (32, GY), 1) < C1
    pair[...] = d_lift
    pack[27 : 27 + 32, :] = jnp.where(low32, pair[pl.ds(0, 32, stride=2), :], pair[pl.ds(1, 32, stride=2), :])

    base = 27 + 32 + 27 * C1
    pack[base : base + C2, :] = d_deep
    base = base + C2
    fine_even_odd = []
    pair[...] = d_fine
    fine_even_odd = [pair[pl.ds(i, 32, stride=2), :] for i in range(2)]
    pair[...] = d_coarse_merge
    coarse_even_odd = [pair[pl.ds(i, 32, stride=2), :] for i in range(2)]
    half = pltpu.roll(coarse_even_odd[0], C1, 1)
    pack[pl.ds(base, 32, stride=3), :] = jnp.where(low32, fine_even_odd[0], half)
    pack[pl.ds(base + 1, 32, stride=3), :] = jnp.where(low32, half, fine_even_odd[1])
    pack[pl.ds(base + 2, 32, stride=3), :] = coarse_even_odd[1]
    base = base + 96
    pack[base : base + 1, :] = jnp.where(lane8[0:1] < C1, d_out[0:1, :], 0.0)
    pack[base + 1 : GROWS, :] = jnp.zeros((GROWS - base - 1, GY), F32)

    per = grad_ref.shape[2]
    for lo in range(grad_ref.shape[0]):
        for hi in range(grad_ref.shape[1]):
            start = (hi * grad_ref.shape[0] + lo) * per
            grad_ref[lo, hi] = pack[start : start + per, :].astype(BF16)
    pred_ref[PZ * PX : PZ * PX + 16, :] = jnp.full((16, GY), slot_ref[0].astype(F32))


def train(scale, n_hi, n_lo, slot, patch, weights):
    cells = PZ * PX * GY
    small = cells // 4
    return pl.pallas_call(
        functools.partial(train_kernel, scale),
        out_shape=(
            jax.ShapeDtypeStruct((PZ * PX + 16, GY), F32),
            jax.ShapeDtypeStruct((n_lo, n_hi, GROWS // (n_lo * n_hi), GY), BF16),
        ),
        in_specs=[SMEM] + [VMEM] * 7,
        out_specs=(VMEM, VMEM),
        scratch_shapes=[
            pltpu.VMEM((PZ * PX * C1, GY), F32),
            pltpu.VMEM((C1, cells), BF16),
            pltpu.VMEM((C1, cells), BF16),
            pltpu.VMEM((C1, cells), BF16),
            pltpu.VMEM((C1, cells), F32),
            pltpu.VMEM((C1, cells), F32),
            pltpu.VMEM((C1, cells), F32),
            pltpu.VMEM((28 * C1, small), BF16),
            pltpu.VMEM((9 * C2, small), BF16),
            pltpu.VMEM((3 * C1, 9 * C2), BF16),
            pltpu.VMEM((GROWS, GY), F32),
            pltpu.VMEM((C1, GY), F32),
        ],
        compiler_params=pltpu.CompilerParams(vmem_limit_bytes=48 * 2**20),
        name="train",
    )(slot, patch, *weights)


def share_kernel(
    n_sec,
    n_hi,
    n_lo,
    g_ref,
    p_ref,
    pred_out,
    grad_out,
    packet,
    buf1,
    acc,
    buf2,
    pbuf,
    q_ref,
    qbuf,
    s1,
    r1,
    s2,
    r2,
    s3,
    r3,
    s4,
    r4,
):
    sec = lax.axis_index("section")
    dp = lax.axis_index("dp")
    hi = lax.div(dp, n_lo)
    lo = lax.rem(dp, n_lo)
    across = n_sec * n_hi
    mine = sec * n_hi + hi

    def in_line(d):
        peer = lax.rem(lo + d, n_lo)
        return peer, (sec, hi * n_lo + peer)

    def in_column(d):
        peer = lax.rem(mine + d, across)
        return peer, (lax.div(peer, n_hi), lax.rem(peer, n_hi) * n_lo + lo)

    def in_part(d):
        peer = lax.rem(hi + d, n_hi)
        return peer, (sec, peer * n_lo + lo)

    barrier = pltpu.get_barrier_semaphore()
    for d in range(1, n_lo):
        pl.semaphore_signal(barrier, inc=1, device_id=in_line(d)[1], device_id_type=MESH)
    for d in range(1, across):
        pl.semaphore_signal(barrier, inc=1, device_id=in_column(d)[1], device_id_type=MESH)
    packet[...] = p_ref[...].astype(BF16)
    pl.semaphore_wait(barrier, n_lo - 1 + across - 1)

    def send(src, dst, ssem, rsem, device):
        copy = pltpu.make_async_remote_copy(
            src_ref=src, dst_ref=dst, send_sem=ssem, recv_sem=rsem, device_id=device, device_id_type=MESH
        )
        copy.start()
        return copy

    grads = []
    for d in range(1, n_lo):
        peer, device = in_line(d)
        grads.append(send(g_ref.at[peer], buf1.at[d - 1], s1.at[d - 1], r1.at[d - 1], device))
    packets = []
    for d in range(1, n_hi):
        peer, device = in_part(d)
        packets.append(send(packet, pbuf.at[d], s3.at[d - 1], r3.at[d - 1], device))
    pbuf[0] = packet[...]
    for copy in grads:
        copy.wait_recv()

    def add_line(h, carry):
        value = g_ref[lo, h].astype(F32)
        for d in range(n_lo - 1):
            value = value + buf1[d, h].astype(F32)
        acc[h] = value
        return carry

    lax.fori_loop(0, n_hi, add_line, 0)
    partials = []
    for d in range(1, across):
        peer, device = in_column(d)
        partials.append(
            send(acc.at[lax.rem(peer, n_hi)], buf2.at[mine], s2.at[d - 1], r2.at[d - 1], device)
        )
    buf2[mine] = acc[hi]

    for copy in packets:
        copy.wait_recv()
    cells = PZ * PX

    def route(q, carry):
        wanted = (hi * (2 * n_lo) + q).astype(F32)
        value = jnp.zeros((cells, GY), F32)
        for src in range(n_hi):
            named = pbuf[src, cells : cells + 16, :].astype(F32)
            named = jnp.concatenate([named] * (cells // 16), axis=0)
            value = value + jnp.where(named == wanted, pbuf[src, 0:cells, :].astype(F32), 0.0)
        q_ref[q] = value.astype(BF16)
        return carry

    lax.fori_loop(0, 2 * n_lo, route, 0)
    routed = []
    for d in range(1, n_lo):
        peer, device = in_line(d)
        routed.append(send(q_ref.at[pl.ds(2 * peer, 2)], qbuf.at[d - 1], s4.at[d - 1], r4.at[d - 1], device))

    for copy in partials:
        copy.wait_recv()

    def add_column(t, total):
        return total + buf2[t]

    grad_out[...] = lax.fori_loop(1, across, add_column, buf2[0])

    for copy in routed:
        copy.wait_recv()
    for s in range(2):
        value = q_ref[2 * lo + s].astype(F32)
        for d in range(n_lo - 1):
            value = value + qbuf[d, s].astype(F32)
        for z in range(PZ):
            pred_out[s, z] = value[z * PX : (z + 1) * PX].astype(BF16)
    for copy in grads + packets + partials + routed:
        copy.wait_send()


def share(n_sec, n_hi, n_lo, grads, preds):
    per = grads.shape[2]
    across = n_sec * n_hi
    dma = pltpu.SemaphoreType.DMA
    return pl.pallas_call(
        functools.partial(share_kernel, n_sec, n_hi, n_lo),
        out_shape=(
            jax.ShapeDtypeStruct((2, PZ, PX, GY), BF16),
            jax.ShapeDtypeStruct((per, GY), F32),
        ),
        in_specs=[VMEM, VMEM],
        out_specs=(VMEM, VMEM),
        scratch_shapes=[
            pltpu.VMEM((PZ * PX + 16, GY), BF16),
            pltpu.VMEM((n_lo - 1, n_hi, per, GY), BF16),
            pltpu.VMEM((n_hi, per, GY), F32),
            pltpu.VMEM((across, per, GY), F32),
            pltpu.VMEM((n_hi, PZ * PX + 16, GY), BF16),
            pltpu.VMEM((2 * n_lo, PZ * PX, GY), BF16),
            pltpu.VMEM((n_lo - 1, 2, PZ * PX, GY), BF16),
            dma((n_lo - 1,)),
            dma((n_lo - 1,)),
            dma((across - 1,)),
            dma((across - 1,)),
            dma((n_hi - 1,)),
            dma((n_hi - 1,)),
            dma((n_lo - 1,)),
            dma((n_lo - 1,)),
        ],
        compiler_params=pltpu.CompilerParams(
            collective_id=1, has_side_effects=True, vmem_limit_bytes=16 * 2**20
        ),
        name="share",
    )(grads, preds)


def local(
    n_sec,
    n_dp,
    heat_start,
    conductivity,
    patch_z,
    patch_x,
    slot_table,
    w_stem,
    w_lift,
    w_down,
    w_deep,
    w_merge,
    w_out,
):
    n_lo = LINE
    n_hi = n_dp // n_lo
    weights = (w_stem, w_lift, w_down, w_deep, w_merge, w_out)
    heat_two, patch = heat_steps(n_sec, n_dp, heat_start, conductivity, patch_z, patch_x)
    scale = 1.0 / (n_sec * n_dp * PZ * PX * GY)
    preds, grads = train(scale, n_hi, n_lo, slot_table, patch, weights)
    predictions, grad_pack = share(n_sec, n_hi, n_lo, grads, preds)
    return heat_two, predictions, grad_pack


def solution(mesh):
    n_sec, n_dp = mesh.shape["section"], mesh.shape["dp"]
    both = ("section", "dp")
    return jax.shard_map(
        functools.partial(local, n_sec, n_dp),
        mesh=mesh,
        in_specs=(P(both, None, None), P(both, None, None), P(both), P(both), P(both)) + (P(),) * 6,
        out_specs=(P(both, None, None), P(both, None, None, None), P("dp", None)),
        check_vma=False,
    )
```

time: 1030 us -> 53.5 us (0.05); the launches traced: 1020 us -> 53.2 us
  waiting for transfers between devices: 559 us -> 0 us
  local copies, waits for them, and re-layouts: 214 us -> 5.37 us
  blocking collectives: 84.2 us -> 0 us
  other arithmetic: 64.5 us -> 0 us
  Pallas kernels: 0 us -> 45.2 us
  matrix products: 38.5 us -> 0 us
  starting transfers between devices: 37.5 us -> 0 us
  between operations: 17.2 us -> 2.65 us
    reduce_scatter x1 -> x0, waiting for transfers between devices: 557 us -> none  [local(): grad_shard = lax.psum_scatter(packed, 'dp', scatter_dimension=0, tiled=True)]
    split x57 -> x0, local copies, waits for them, and re-layouts: 98.6 us -> none  [the longest x56 97.2 us: conv_cube(): columns = jnp.concatenate(shifted, axis=0)]
    unnamed x1 -> x0, blocking collectives: 77 us -> none
    unnamed x129 -> x19, local copies, waits for them, and re-layouts: 70.5 us -> 5.37 us
    pallas_call x0 -> x3, Pallas kernels: none -> 45.2 us  [the longest x1 22.1 us: share(): pl.pallas_call(functools.partial(share_kernel, n_sec, n_hi, n_lo), out_sh...]
    dot_general x17 -> x0, matrix products: 38.5 us -> none  [the longest x5 18.2 us: conv_cube(): jnp.dot(kernel, columns.reshape(columns.shape[0], -1), preferred_element_...]
    mul x2 -> x0, other arithmetic: 27.3 us -> none  [local(): outgoing = sender_mask * own_patch.reshape(1, -1)]
    all_to_all x1 -> x0, starting transfers between devices: 24.5 us -> none  [local(): lax.all_to_all(outgoing, 'dp', split_axis=0, concat_axis=0, tiled=True)]
  transfers between devices with their start and end apart: 6 -> 0, of which waited for: 3 -> 0; matrix products, arithmetic and copies ran while one was open for 0% -> 0% of each run, Pallas kernels for 0% -> 0%
where the time goes in v1:
time: 53.5 us; the launch traced here: 53.2 us
  Pallas kernels  45.2 us (84%)
  local copies, waits for them, and re-layouts  5.37 us (10%)
  between operations  2.65 us (5%)
    pallas_call x1, Pallas kernels, share(): pl.pallas_call(functools.partial(share_kernel, n_sec, n_hi, n_lo), out_sh...  22.1 us
    pallas_call x1, Pallas kernels, heat_steps(): pl.pallas_call(functools.partial(heat_kernel, n_sec, n_dp), out_shape=(ja...  14.7 us
    pallas_call x1, Pallas kernels, train(): pl.pallas_call(functools.partial(train_kernel, scale), out_shape=(jax.Sha...  8.48 us
    unnamed x19, local copies, waits for them, and re-layouts  5.37 us

profile of v1, /device:TPU:1, one launch (start us, length us, event | category | flops | bytes accessed | tf_op | source)
XLA Modules:
  0.0 53.2 jit_solution(18009819079986795658)
XLA Ops:
  2.6 0.8 %copy.14.w_stem = bf16[64,54]{1,0:T(8,128)(2,1)S(1)} copy(bf16[64,54]{0,1:T(8,128)(2,1)} %param.16) | data formatting | bytes 13824 | tf_op args[5]
  3.4 0.0 copy-start
  3.4 0.9 %copy-done = f32[16,32,128]{2,1,0:T(8,128)S(1)} copy-done((f32[16,32,128]{2,1,0:T(8,128)S(1)}, f32[16,32,128]{2,1,0:T(8,128)}, u32[]{:S(2)}) %copy-start) | copy-done | bytes 262168
  4.3 0.0 copy-start.1
  4.3 0.9 %copy-done.1 = f32[16,32,128]{2,1,0:T(8,128)S(1)} copy-done((f32[16,32,128]{2,1,0:T(8,128)S(1)}, f32[16,32,128]{2,1,0:T(8,128)}, u32[]{:S(2)}) %copy-start.1) | copy-done | bytes 262168
  5.3 0.0 copy-start.6
  5.3 14.7 %heat.1 = (f32[16,32,128]{2,1,0:T(8,128)S(1)}, f32[3,4,8,128]{3,2,1,0:T(8,128)S(1)}) custom-call(s32[1]{0:T(128)S(6)} %copy.19.pz_ref, s32[1]{0:T(128)S(6)} %copy.20.px_ref, f32[16,32,128]{2,1,0:T(8,128)S(1)} %copy-done, f32[16,32,128]{2,1,0:T(8,128)S(1)} %copy-done.1), custom_call_target="tpu_custom_call" | custom-call | tf_op jit(solution)/shard_map/heat/pallas_call | solution.py:119
  20.0 0.0 copy-done.6
  20.0 0.0 copy-start.2
  20.0 0.0 copy-start.3
  20.0 0.0 copy-start.4
  20.0 0.0 copy-start.5
  20.0 0.2 copy.15.w_down
  20.2 0.5 copy-done.2
  20.7 0.0 copy-done.3
  20.8 0.0 copy-done.4
  20.8 0.0 copy-done.5
  20.8 8.5 %train.1 = (f32[48,128]{1,0:T(8,128)S(1)}, bf16[8,16,16,128]{3,2,1,0:T(8,128)(2,1)S(1)}) custom-call(s32[1]{0:T(128)S(6)} %copy.21.slot_ref, f32[3,4,8,128]{3,2,1,0:T(8,128)S(1)} %get-tuple-element.10.patch_ref, bf16[64,54]{1,0:T(8,128)(2,1)S(1)} %copy.14.w_stem, bf16[64,64]{1,0:T(8,128)(2,1)S(1)} %copy-done.4, bf16[128,1728]{1,0:T(8,128)(2,1)S(1)} %copy.15.w_down, ...), custom_call_target="tpu_custom_call" | custom-call | tf_op jit(solution)/shard_map/train/pallas_call | solution.py:415
  29.2 22.1 %share.1 = (bf16[2,4,8,128]{3,2,1,0:T(8,128)(2,1)S(1)}, f32[16,128]{1,0:T(8,128)S(1)}) custom-call(bf16[8,16,16,128]{3,2,1,0:T(8,128)(2,1)S(1)} %get-tuple-element.11.g_ref, f32[48,128]{1,0:T(8,128)S(1)} %get-tuple-element.12.p_ref), custom_call_target="tpu_custom_call" | custom-call | tf_op jit(solution)/shard_map/share/pallas_call | solution.py:572
  51.3 0.7 %copy.22 = f32[16,32,128]{2,1,0:T(8,128)} copy(f32[16,32,128]{2,1,0:T(8,128)S(1)} %get-tuple-element.18) | data formatting | bytes 524288
  52.0 0.6 %copy.23 = bf16[2,4,8,128]{3,2,1,0:T(8,128)(2,1)} copy(bf16[2,4,8,128]{3,2,1,0:T(8,128)(2,1)S(1)} %get-tuple-element.19) | data formatting | bytes 32768
  52.6 0.6 %copy.24 = f32[16,128]{1,0:T(8,128)} copy(f32[16,128]{1,0:T(8,128)S(1)} %get-tuple-element.20) | data formatting | bytes 16384
Async XLA Ops:
  3.4 1.0 %copy-start = (f32[16,32,128]{2,1,0:T(8,128)S(1)}, f32[16,32,128]{2,1,0:T(8,128)}, u32[]{:S(2)}) copy-start(f32[16,32,128]{2,1,0:T(8,128)} %u_ref.1) | copy-start | bytes 786436
  4.3 0.9 %copy-start.1 = (f32[16,32,128]{2,1,0:T(8,128)S(1)}, f32[16,32,128]{2,1,0:T(8,128)}, u32[]{:S(2)}) copy-start(f32[16,32,128]{2,1,0:T(8,128)} %k_ref.1) | copy-start | bytes 786436
  5.3 14.7 %copy-start.6 = (bf16[128,1728]{0,1:T(8,128)(2,1)S(1)}, bf16[128,1728]{0,1:T(8,128)(2,1)}, u32[]{:S(2)}) copy-start(bf16[128,1728]{0,1:T(8,128)(2,1)} %param.18) | copy-start | bytes 1327108
  20.0 0.8 %copy-start.2 = (bf16[128,128]{1,0:T(8,128)(2,1)S(1)}, bf16[128,128]{1,0:T(8,128)(2,1)}, u32[]{:S(2)}) copy-start(bf16[128,128]{1,0:T(8,128)(2,1)} %w_deep.1) | copy-start | bytes 98308
  20.0 0.8 %copy-start.3 = (bf16[64,192]{1,0:T(8,128)(2,1)S(1)}, bf16[64,192]{1,0:T(8,128)(2,1)}, u32[]{:S(2)}) copy-start(bf16[64,192]{1,0:T(8,128)(2,1)} %w_merge.1) | copy-start | bytes 73732
  20.0 0.8 %copy-start.4 = (bf16[64,64]{1,0:T(8,128)(2,1)S(1)}, bf16[64,64]{1,0:T(8,128)(2,1)}, u32[]{:S(2)}) copy-start(bf16[64,64]{1,0:T(8,128)(2,1)} %w_lift.1) | copy-start | bytes 24580
  20.0 0.7 %copy-start.5 = (bf16[1,64]{1,0:T(2,128)(2,1)S(1)}, bf16[1,64]{1,0:T(2,128)(2,1)}, u32[]{:S(2)}) copy-start(bf16[1,64]{1,0:T(2,128)(2,1)} %w_out.1) | copy-start | bytes 388

commit v2 on v1

v2 whole, which is shorter than its diff:
```python
import functools

import jax
import jax.numpy as jnp
from jax import lax
from jax.experimental import pallas as pl
from jax.experimental.pallas import tpu as pltpu
from jax.sharding import PartitionSpec as P

MESH = pl.DeviceIdType.MESH
TIME_STEP = 0.15
GY = 128
PZ = 4
PX = 8
C1 = 64
C2 = 128
GROWS = 2048
LINE = 8
F32 = jnp.float32
BF16 = jnp.bfloat16
VMEM = pl.BlockSpec(memory_space=pltpu.VMEM)
SMEM = pl.BlockSpec(memory_space=pltpu.SMEM)
HBM = pl.BlockSpec(memory_space=pltpu.HBM)


def rounded(x):
    return x.astype(BF16).astype(F32)


NT = (((1,), (1,)), ((), ()))
NN = (((1,), (0,)), ((), ()))


def mm(a, b, dims=NN):
    return lax.dot_general(a, b, dims, preferred_element_type=F32)


def heat_kernel(
    n_sec,
    n_dp,
    pz_ref,
    px_ref,
    u_hbm,
    k_hbm,
    stem_hbm,
    lift_hbm,
    down_hbm,
    deep_hbm,
    merge_hbm,
    proj_hbm,
    out_ref,
    patch_ref,
    stem_ref,
    lift_ref,
    lift_t,
    down_ref,
    down_back,
    deep_ref,
    deep_t,
    fine_ref,
    fine_t,
    coarse_ref,
    coarse_t,
    proj_ref,
    proj_col,
    v_stem,
    v_down,
    v_merge,
    v_proj,
    u_ref,
    k_ref,
    ulo,
    klo,
    uhi,
    khi,
    h1,
    load,
    send,
    recv,
):
    total = n_sec * n_dp
    depth = u_ref.shape[0]
    me = lax.axis_index("section") * n_dp + lax.axis_index("dp")
    after = lax.rem(me + 1, total)
    before = lax.rem(me + total - 1, total)

    def place(i):
        return (lax.div(i, n_dp), lax.rem(i, n_dp))

    barrier = pltpu.get_barrier_semaphore()
    for peer in (before, after):
        pl.semaphore_signal(barrier, inc=1, device_id=place(peer), device_id_type=MESH)
    loads = [
        pltpu.make_async_copy(u_hbm, u_ref, load.at[0]),
        pltpu.make_async_copy(k_hbm, k_ref, load.at[1]),
        pltpu.make_async_copy(down_hbm, v_down, load.at[2]),
        pltpu.make_async_copy(stem_hbm, v_stem, load.at[3]),
        pltpu.make_async_copy(lift_hbm, lift_ref, load.at[4]),
        pltpu.make_async_copy(deep_hbm, deep_ref, load.at[5]),
        pltpu.make_async_copy(merge_hbm, v_merge, load.at[6]),
        pltpu.make_async_copy(proj_hbm, v_proj, load.at[7]),
    ]
    for copy in loads:
        copy.start()
    pl.semaphore_wait(barrier, 2)
    plan = (
        (u_hbm.at[pl.ds(depth - 2, 2)], ulo, after),
        (u_hbm.at[pl.ds(0, 2)], uhi, before),
        (k_hbm.at[pl.ds(depth - 2, 2)], klo, after),
        (k_hbm.at[pl.ds(0, 2)], khi, before),
    )
    copies = []
    for i, (src, dst, peer) in enumerate(plan):
        copy = pltpu.make_async_remote_copy(
            src_ref=src,
            dst_ref=dst,
            send_sem=send.at[i],
            recv_sem=recv.at[i],
            device_id=place(peer),
            device_id_type=MESH,
        )
        copy.start()
        copies.append(copy)

    rows, lanes = u_ref.shape[1:]
    row = lax.broadcasted_iota(jnp.int32, (rows, lanes), 0)
    lane = lax.broadcasted_iota(jnp.int32, (rows, lanes), 1)

    def step(up, uc, un, kp, kc, kn):
        flux = (kc + kn) * (un - uc) + (kc + kp) * (up - uc)
        for axis, place_, size in ((0, row, rows), (1, lane, lanes)):
            last = place_ == size - 1
            first = place_ == 0
            u_next = jnp.where(last, 0.0, pltpu.roll(uc, size - 1, axis))
            k_next = jnp.where(last, 0.0, pltpu.roll(kc, size - 1, axis))
            face = (kc + k_next) * (u_next - uc)
            back = jnp.where(first, kc * uc, pltpu.roll(face, 1, axis))
            flux = flux + (face - back)
        return uc + (0.5 * TIME_STEP) * flux

    for copy in loads:
        copy.wait()
    group = 7

    def interior(i, carry):
        for j in range(group):
            z = 1 + i * group + j
            h1[z + 1] = step(
                u_ref[z - 1], u_ref[z], u_ref[z + 1], k_ref[z - 1], k_ref[z], k_ref[z + 1]
            )
        return carry

    lax.fori_loop(0, (depth - 2) // group, interior, 0)

    def second(z):
        out_ref[z] = step(h1[z], h1[z + 1], h1[z + 2], k_ref[z - 1], k_ref[z], k_ref[z + 1])

    pack = 6

    def inner(i, carry):
        for j in range(pack):
            second(2 + i * pack + j)
        return carry

    lax.fori_loop(0, (depth - 4) // pack, inner, 0)
    unit = lax.broadcasted_iota(jnp.int32, (C2, C2), 0) == lax.broadcasted_iota(jnp.int32, (C2, C2), 1)
    eye = unit[0:C1, 0:C1]
    unit = unit.astype(BF16)
    stem_ref[...] = mm(unit[0:C1, 0:C1], v_stem[...], NT).astype(BF16)
    down_ref[...] = mm(unit, v_down[...], NT).astype(BF16)
    for j in range(9):
        down_back[:, j * C2 : (j + 1) * C2] = v_down[j * 3 * C1 : (j + 1) * 3 * C1, :]

    def turned(x):
        return x.astype(F32).T.astype(BF16)

    lift_t[...] = turned(lift_ref[...])
    deep_t[...] = turned(deep_ref[...])
    fine = v_merge[:, 0:C1]
    coarse = v_merge[:, C1 : C1 + C2]
    fine_ref[...] = fine
    fine_t[...] = turned(fine)
    coarse_ref[...] = coarse
    coarse_t[...] = turned(coarse)
    row64 = v_proj[...].astype(F32)
    proj_ref[...] = jnp.broadcast_to(row64, proj_ref.shape).astype(BF16)
    column = jnp.sum(jnp.where(eye, jnp.broadcast_to(row64, (C1, C1)), 0.0), axis=1, keepdims=True)
    proj_col[...] = jnp.broadcast_to(column, proj_col.shape)

    for copy in copies:
        copy.wait_recv()
    has_lo = (me > 0).astype(F32)
    has_hi = (me < total - 1).astype(F32)
    ul = [ulo[0] * has_lo, ulo[1] * has_lo]
    kl = [klo[0] * has_lo, klo[1] * has_lo]
    uh = [uhi[0] * has_hi, uhi[1] * has_hi]
    kh = [khi[0] * has_hi, khi[1] * has_hi]
    end = depth - 1
    h1[0] = has_lo * step(ul[0], ul[1], u_ref[0], kl[0], kl[1], k_ref[0])
    h1[1] = step(ul[1], u_ref[0], u_ref[1], kl[1], k_ref[0], k_ref[1])
    h1[depth] = step(u_ref[end - 1], u_ref[end], uh[0], k_ref[end - 1], k_ref[end], kh[0])
    h1[depth + 1] = has_hi * step(u_ref[end], uh[0], uh[1], k_ref[end], kh[0], kh[1])

    out_ref[0] = step(h1[0], h1[1], h1[2], kl[1], k_ref[0], k_ref[1])
    out_ref[end] = step(h1[end], h1[depth], h1[depth + 1], k_ref[end - 1], k_ref[end], kh[0])
    second(1)
    second(end - 1)
    pz = pz_ref[0]
    px = px_ref[0]
    for z in range(PZ):
        patch_ref[0, z] = h1[1 + pz + z, pl.ds(px, PX), :]
        patch_ref[1, z] = k_ref[pz + z, pl.ds(px, PX), :]
        patch_ref[2, z] = out_ref[pz + z, pl.ds(px, PX), :]
    for copy in copies:
        copy.wait_send()


def heat_steps(n_sec, n_dp, heat, cond, patch_z, patch_x, weights):
    layers = (2,) + heat.shape[1:]
    taps = weights[0].shape[0]
    return pl.pallas_call(
        functools.partial(heat_kernel, n_sec, n_dp),
        out_shape=(
            jax.ShapeDtypeStruct(heat.shape, F32),
            jax.ShapeDtypeStruct((3, PZ, PX, GY), F32),
            jax.ShapeDtypeStruct((C1, taps), BF16),
            jax.ShapeDtypeStruct((C1, C1), BF16),
            jax.ShapeDtypeStruct((C1, C1), BF16),
            jax.ShapeDtypeStruct((C2, 27 * C1), BF16),
            jax.ShapeDtypeStruct((3 * C1, 9 * C2), BF16),
            jax.ShapeDtypeStruct((C2, C2), BF16),
            jax.ShapeDtypeStruct((C2, C2), BF16),
            jax.ShapeDtypeStruct((C1, C1), BF16),
            jax.ShapeDtypeStruct((C1, C1), BF16),
            jax.ShapeDtypeStruct((C1, C2), BF16),
            jax.ShapeDtypeStruct((C2, C1), BF16),
            jax.ShapeDtypeStruct((16, C1), BF16),
            jax.ShapeDtypeStruct((C1, GY), F32),
        ),
        in_specs=[SMEM, SMEM] + [HBM] * 8,
        out_specs=(VMEM,) * 15,
        scratch_shapes=[
            pltpu.VMEM(weights[0].shape, BF16),
            pltpu.VMEM(weights[2].shape, BF16),
            pltpu.VMEM(weights[4].shape, BF16),
            pltpu.VMEM(weights[5].shape, BF16),
            pltpu.VMEM(heat.shape, F32),
            pltpu.VMEM(heat.shape, F32),
            pltpu.VMEM(layers, F32),
            pltpu.VMEM(layers, F32),
            pltpu.VMEM(layers, F32),
            pltpu.VMEM(layers, F32),
            pltpu.VMEM((heat.shape[0] + 2,) + heat.shape[1:], F32),
            pltpu.SemaphoreType.DMA((8,)),
            pltpu.SemaphoreType.DMA((4,)),
            pltpu.SemaphoreType.DMA((4,)),
        ],
        compiler_params=pltpu.CompilerParams(
            collective_id=0, has_side_effects=True, vmem_limit_bytes=16 * 2**20
        ),
        name="heat",
    )(patch_z, patch_x, *[pltpu.with_memory_space_constraint(x, pltpu.HBM) for x in (heat, cond, *weights)])


def silu_and_slope(z):
    s = 0.5 * jnp.tanh(0.5 * z) + 0.5
    value = z * s
    return value, s + value * (1.0 - s)


def block(x, b):
    return x[:, b * GY : (b + 1) * GY]


def train_kernel(
    scale,
    n_sec,
    n_hi,
    n_lo,
    slot_ref,
    patch_ref,
    w_stem,
    w_lift,
    w_lift_t,
    w_down,
    wback,
    w_deep,
    w_deep_t,
    w_fine,
    w_fine_t,
    w_coarse,
    w_coarse_t,
    w_proj,
    w_proj_col,
    pred_out,
    buf2,
    tall,
    cols,
    l1,
    l2,
    g1,
    g2,
    merged_ref,
    dz_ref,
    colsd,
    colsz,
    pack,
    pair,
    grads,
    packet,
    buf1,
    acc,
    pbuf,
    q_ref,
    qbuf,
    s1,
    r1,
    s1b,
    r1b,
    s2,
    r2,
    s3,
    r3,
    s4,
    r4,
):
    sec = lax.axis_index("section")
    dp = lax.axis_index("dp")
    hi = lax.div(dp, n_lo)
    lo = lax.rem(dp, n_lo)
    across = n_sec * n_hi
    mine = sec * n_hi + hi

    def in_line(d):
        peer = lax.rem(lo + d, n_lo)
        return peer, (sec, hi * n_lo + peer)

    def in_column(d):
        peer = lax.rem(mine + d, across)
        return peer, (lax.div(peer, n_hi), lax.rem(peer, n_hi) * n_lo + lo)

    def in_part(d):
        peer = lax.rem(hi + d, n_hi)
        return peer, (sec, peer * n_lo + lo)

    def send(src, dst, ssem, rsem, device):
        copy = pltpu.make_async_remote_copy(
            src_ref=src, dst_ref=dst, send_sem=ssem, recv_sem=rsem, device_id=device, device_id_type=MESH
        )
        copy.start()
        return copy

    barrier = pltpu.get_barrier_semaphore()
    for d in range(1, across):
        pl.semaphore_signal(barrier, inc=1, device_id=in_column(d)[1], device_id_type=MESH)
    for d in range(1, n_lo):
        pl.semaphore_signal(barrier, inc=1, device_id=in_line(d)[1], device_id_type=MESH)

    plane = PX * GY
    cells = PZ * plane
    small = cells // 4
    row8 = lax.broadcasted_iota(jnp.int32, (PX, GY), 0)
    lane8 = lax.broadcasted_iota(jnp.int32, (PX, GY), 1)
    lane64 = lax.broadcasted_iota(jnp.int32, (C1, GY), 1)

    tall[...] = jnp.zeros_like(tall)
    for channel in range(2):
        for dx in range(3):
            for dy in range(3):
                shifted = []
                for z in range(PZ):
                    v = rounded(patch_ref[channel, z])
                    if dx == 0:
                        v = jnp.where(row8 == 0, 0.0, pltpu.roll(v, 1, 0))
                    elif dx == 2:
                        v = jnp.where(row8 == PX - 1, 0.0, pltpu.roll(v, PX - 1, 0))
                    if dy == 0:
                        v = jnp.where(lane8 == 0, 0.0, pltpu.roll(v, 1, 1))
                    elif dy == 2:
                        v = jnp.where(lane8 == GY - 1, 0.0, pltpu.roll(v, GY - 1, 1))
                    shifted.append(v)
                for dz in range(3):
                    r = ((dz * 3 + dx) * 3 + dy) * 2 + channel
                    for z in range(PZ):
                        if 0 <= z + dz - 1 < PZ:
                            tall[pl.ds(z * PX * C1 + r, PX, stride=C1), :] = shifted[z + dz - 1]
    for b in range(PZ * PX):
        cols[:, b * GY : (b + 1) * GY] = tall[b * C1 : (b + 1) * C1, :].astype(BF16)

    taps = w_stem.shape[1]
    depth = 27 * C1
    stem = w_stem[...]
    lift = w_lift[...]
    pooled = []
    for zz in range(PZ // 2):
        rows = []
        for z in (2 * zz, 2 * zz + 1):
            here = slice(z * plane, (z + 1) * plane)
            value, slope = silu_and_slope(mm(stem, cols[0:taps, here]))
            g1[:, here] = slope
            one = value.astype(BF16)
            l1[:, here] = one
            value, slope = silu_and_slope(mm(lift, one))
            g2[:, here] = slope
            two = value.astype(BF16)
            l2[:, here] = two
            rows.append(two.astype(F32))
        both = rows[0] + rows[1]
        for xx in range(PX // 2):
            pooled.append(rounded((block(both, 2 * xx) + block(both, 2 * xx + 1)) * 0.25))

    hz, hx = PZ // 2, PX // 2
    shifted = []
    for dy in range(3):
        if dy == 0:
            part = [jnp.where(lane64 == 0, 0.0, pltpu.roll(v, 1, 1)) for v in pooled]
        elif dy == 1:
            part = pooled
        else:
            part = [jnp.where(lane64 == GY - 1, 0.0, pltpu.roll(v, GY - 1, 1)) for v in pooled]
        shifted.append([v.astype(BF16) for v in part])
    nothing = jnp.zeros((C1, GY), BF16)
    for dz in range(3):
        for dx in range(3):
            for dy in range(3):
                r = ((dz * 3 + dx) * 3 + dy) * C1
                for z in range(hz):
                    for x in range(hx):
                        sz, sx = z + dz - 1, x + dx - 1
                        inside = 0 <= sz < hz and 0 <= sx < hx
                        b = z * hx + x
                        colsd[r : r + C1, b * GY : (b + 1) * GY] = (
                            shifted[dy][sz * hx + sx] if inside else nothing
                        )
    colsd[depth : depth + C1, :] = jnp.zeros((C1, small), BF16)
    value, slope_down = silu_and_slope(mm(w_down[...], colsd[0:depth, :]))
    coarse = value.astype(BF16)
    value, slope_deep = silu_and_slope(mm(w_deep[...], coarse))
    deeper = value.astype(BF16)
    merge_fine = w_fine[...]
    lifted = mm(w_coarse[...], deeper)

    out_col = w_proj_col[...]
    out8 = w_proj[0:8, :]
    fine_t = w_fine_t[...]
    slim = []
    gathered = [None] * (hz * hx)
    forecast = []
    for z in range(PZ):
        here = slice(z * plane, (z + 1) * plane)
        two = l2[:, here]
        added = [block(lifted, (z // 2) * hx + x // 2) for x in range(PX)]
        value, slope = silu_and_slope(mm(merge_fine, two) + jnp.concatenate(added, axis=1))
        merged = value.astype(BF16)
        wide = mm(out8, merged)
        predicted = jnp.zeros((PX, GY), F32)
        for x in range(PX):
            predicted = jnp.where(row8 == x, block(wide, x), predicted)
        forecast.append(predicted)
        misfit = (predicted - rounded(patch_ref[2, z])) * scale
        d_wide = jnp.concatenate(
            [jnp.broadcast_to(misfit[x : x + 1, :], (8, GY)) for x in range(PX)], axis=1
        ).astype(BF16)
        merged_ref[:, here] = merged
        d_merged = jnp.concatenate([out_col * misfit[x : x + 1, :] for x in range(PX)], axis=1)
        dz = rounded(d_merged) * slope
        for x in range(PX):
            b = (z // 2) * hx + x // 2
            gathered[b] = block(dz, x) if gathered[b] is None else gathered[b] + block(dz, x)
        dz = dz.astype(BF16)
        dz_ref[:, here] = dz
        slim.append(d_wide)

    half = PZ * PX // 2
    packet[0:half, :] = jnp.concatenate(forecast[0 : PZ // 2], axis=0).astype(BF16)
    packet[half : 2 * half, :] = jnp.concatenate(forecast[PZ // 2 : PZ], axis=0).astype(BF16)
    packet[2 * half : 2 * half + 16, :] = jnp.full((16, GY), slot_ref[0].astype(F32)).astype(BF16)
    pl.semaphore_wait(barrier, n_lo - 1 + across - 1)
    packets = []
    for d in range(1, n_hi):
        peer, device = in_part(d)
        packets.append(send(packet, pbuf.at[d], s3.at[d - 1], r3.at[d - 1], device))
    pbuf[0] = packet[...]

    d_lifted = jnp.concatenate(gathered, axis=1).astype(BF16)
    d_deeper = mm(w_coarse_t[...], d_lifted)
    dz_deep = (rounded(d_deeper) * slope_deep).astype(BF16)
    d_coarse = mm(w_deep_t[...], dz_deep)
    dz_down = (rounded(d_coarse) * slope_down).astype(BF16)

    r_ = lax.broadcasted_iota(jnp.int32, (C2, C2), 0)
    c_ = lax.broadcasted_iota(jnp.int32, (C2, C2), 1)
    parted = jnp.where(r_ < C1, 2 * r_, 2 * r_ - (C2 - 1)) == c_
    dz_parted = mm(parted.astype(BF16), dz_down).astype(BF16)
    base = 27 + 32
    chunks = [mm(dz_parted, colsd[j * C2 : (j + 1) * C2, :], NT) for j in range(14)]
    low = lane64 < C1
    for j in range(13):
        pack[pl.ds(base + j, C1, stride=27), :] = chunks[j][0:C1]
        pack[pl.ds(base + 14 + j, C1, stride=27), :] = pltpu.roll(
            jnp.where(low, chunks[j + 1][C1:C2], chunks[j][C1:C2]), C1, 1
        )
    pack[pl.ds(base + 13, C1, stride=27), :] = jnp.where(
        low, chunks[13][0:C1], pltpu.roll(chunks[0][C1:C2], C1, 1)
    )

    per = grads.shape[2]
    first = -(-(27 + 32) // (per * n_lo))
    top = n_hi - (27 + 32 + 27 * C1) // (per * n_lo)
    tail = first + top

    def emit(hi_):
        for lo_ in range(n_lo):
            start = (hi_ * n_lo + lo_) * per
            grads[lo_, (hi_ + top) % n_hi] = pack[start : start + per, :].astype(BF16)

    for h in range(first, n_hi - top):
        emit(h)
    early = []
    for d in range(1, n_lo):
        peer, device = in_line(d)
        early.append(
            send(
                grads.at[peer, pl.ds(tail, n_hi - tail)],
                buf1.at[d - 1, pl.ds(tail, n_hi - tail)],
                s1.at[d - 1],
                r1.at[d - 1],
                device,
            )
        )

    d_coarse_merge = mm(d_lifted, deeper, NT)
    d_deep = mm(dz_deep, coarse, NT)
    d_fine = jnp.zeros((C1, GY), F32)
    d_out = jnp.zeros((8, GY), F32)
    for z in range(PZ):
        here = slice(z * plane, (z + 1) * plane)
        merged = merged_ref[:, here]
        d_out = d_out + mm(slim[z], jnp.concatenate([merged, merged], axis=0), NT)
        two = l2[:, here]
        d_fine = d_fine + mm(dz_ref[:, here], jnp.concatenate([two, two], axis=0), NT)
    low32 = lax.broadcasted_iota(jnp.int32, (32, GY), 1) < C1
    base = 27 + 32 + 27 * C1
    pack[base : base + C2, :] = d_deep
    base = base + C2
    pair[...] = d_fine
    fine_even_odd = [pair[pl.ds(i, 32, stride=2), :] for i in range(2)]
    pair[...] = d_coarse_merge
    coarse_even_odd = [pair[pl.ds(i, 32, stride=2), :] for i in range(2)]
    turn = pltpu.roll(coarse_even_odd[0], C1, 1)
    pack[pl.ds(base, 32, stride=3), :] = jnp.where(low32, fine_even_odd[0], turn)
    pack[pl.ds(base + 1, 32, stride=3), :] = jnp.where(low32, turn, fine_even_odd[1])
    pack[pl.ds(base + 2, 32, stride=3), :] = coarse_even_odd[1]
    base = base + 96
    pack[base : base + 1, :] = jnp.where(lane8[0:1] < C1, d_out[0:1, :], 0.0)
    pack[base + 1 : GROWS, :] = jnp.zeros((GROWS - base - 1, GY), F32)


    blank = jnp.zeros((C2, GY), BF16)
    for dz in range(3):
        for dx in range(3):
            j = dz * 3 + dx
            for z in range(hz):
                for x in range(hx):
                    sz, sx = z - (dz - 1), x - (dx - 1)
                    inside = 0 <= sz < hz and 0 <= sx < hx
                    b = z * hx + x
                    colsz[j * C2 : (j + 1) * C2, b * GY : (b + 1) * GY] = (
                        block(dz_down, sz * hx + sx) if inside else blank
                    )
    d_shifted = mm(wback[...], colsz[...])
    d_pooled = []
    for b in range(hz * hx):
        whole = block(d_shifted, b)
        total = whole[C1 : 2 * C1]
        total = total + jnp.where(lane64 == GY - 1, 0.0, pltpu.roll(whole[0:C1], GY - 1, 1))
        total = total + jnp.where(lane64 == 0, 0.0, pltpu.roll(whole[2 * C1 : 3 * C1], 1, 1))
        d_pooled.append(rounded(total) * 0.25)

    lift_t = w_lift_t[...]
    d_lift = jnp.zeros((C1, GY), F32)
    d_stem = jnp.zeros((C1, C1), F32)
    for z in range(PZ):
        here = slice(z * plane, (z + 1) * plane)
        spread = jnp.concatenate([d_pooled[(z // 2) * hx + x // 2] for x in range(PX)], axis=1)
        dz = ((rounded(mm(fine_t, dz_ref[:, here])) + spread) * g2[:, here]).astype(BF16)
        one = l1[:, here]
        d_lift = d_lift + mm(dz, jnp.concatenate([one, one], axis=0), NT)
        d_one = rounded(mm(lift_t, dz))
        dz = (d_one * g1[:, here]).astype(BF16)
        d_stem = d_stem + mm(dz, cols[:, here], NT)

    pair[:, 0:C1] = d_stem
    pair[:, C1:GY] = jnp.zeros((C1, GY - C1), F32)
    turned = pair[...]
    source = lax.broadcasted_iota(jnp.int32, (C1, GY), 0)
    for bit in range(6):
        moved = pltpu.roll(turned, (taps << bit) % GY, 1)
        turned = jnp.where((source >> bit) % 2 == 1, moved, turned)
    begin = source * taps
    wraps = lane64 < begin % GY
    stay = jnp.where(wraps, 0.0, turned).astype(BF16)
    over = jnp.where(wraps, turned, 0.0).astype(BF16)
    target_row = lax.broadcasted_iota(jnp.int32, (32, C1), 0)
    owner = lax.broadcasted_iota(jnp.int32, (32, C1), 1) * taps // GY
    stem_rows = mm((target_row == owner).astype(BF16), stay)
    stem_rows = stem_rows + mm((target_row == owner + 1).astype(BF16), over)
    pack[0:27, :] = stem_rows[0:27, :]

    low32 = lax.broadcasted_iota(jnp.int32, (32, GY), 1) < C1
    pair[...] = d_lift
    pack[27 : 27 + 32, :] = jnp.where(low32, pair[pl.ds(0, 32, stride=2), :], pair[pl.ds(1, 32, stride=2), :])


    for h in list(range(first)) + list(range(n_hi - top, n_hi)):
        emit(h)
    late = []
    for d in range(1, n_lo):
        peer, device = in_line(d)
        late.append(
            send(
                grads.at[peer, pl.ds(0, tail)],
                buf1.at[d - 1, pl.ds(0, tail)],
                s1b.at[d - 1],
                r1b.at[d - 1],
                device,
            )
        )

    for copy in packets:
        copy.wait_recv()
    rows = PZ * PX

    def route(q, carry):
        wanted = (hi * (2 * n_lo) + q).astype(F32)
        value = jnp.zeros((rows, GY), F32)
        for src in range(n_hi):
            named = pbuf[src, rows : rows + 16, :].astype(F32)
            named = jnp.concatenate([named] * (rows // 16), axis=0)
            value = value + jnp.where(named == wanted, pbuf[src, 0:rows, :].astype(F32), 0.0)
        q_ref[q] = value.astype(BF16)
        return carry

    lax.fori_loop(0, 2 * n_lo, route, 0)
    routed = []
    for d in range(1, n_lo):
        peer, device = in_line(d)
        routed.append(send(q_ref.at[pl.ds(2 * peer, 2)], qbuf.at[d - 1], s4.at[d - 1], r4.at[d - 1], device))

    for copy in early + late:
        copy.wait_recv()

    partials = []
    for e in range(1, n_hi + 1):
        h = lax.rem(hi + e, n_hi)
        at = lax.rem(h + top, n_hi)
        value = grads[lo, at].astype(F32)
        for d in range(n_lo - 1):
            value = value + buf1[d, at].astype(F32)
        acc[h] = value.astype(BF16)
        for q in range(n_sec):
            if e == n_hi and q == 0:
                buf2[mine] = acc[h]
                continue
            owner = lax.rem(sec + q, n_sec)
            partials.append(
                send(
                    acc.at[h],
                    buf2.at[mine],
                    s2.at[q * n_hi + e - 1],
                    r2.at[q * n_hi + e - 1],
                    (owner, h * n_lo + lo),
                )
            )

    for copy in routed:
        copy.wait_recv()
    for s in range(2):
        value = q_ref[2 * lo + s].astype(F32)
        for d in range(n_lo - 1):
            value = value + qbuf[d, s].astype(F32)
        pred_out[s] = value

    for copy in partials:
        copy.wait_recv()
    for copy in packets + early + late + routed + partials:
        copy.wait_send()


def train(scale, n_sec, n_hi, n_lo, slot, patch, weights):
    cells = PZ * PX * GY
    small = cells // 4
    per = GROWS // (n_lo * n_hi)
    across = n_sec * n_hi
    dma = pltpu.SemaphoreType.DMA
    return pl.pallas_call(
        functools.partial(train_kernel, scale, n_sec, n_hi, n_lo),
        out_shape=(
            jax.ShapeDtypeStruct((2, PZ * PX, GY), F32),
            jax.ShapeDtypeStruct((across, per, GY), BF16),
        ),
        in_specs=[SMEM] + [VMEM] * 14,
        out_specs=(VMEM, VMEM),
        scratch_shapes=[
            pltpu.VMEM((PZ * PX * C1, GY), F32),
            pltpu.VMEM((C1, cells), BF16),
            pltpu.VMEM((C1, cells), BF16),
            pltpu.VMEM((C1, cells), BF16),
            pltpu.VMEM((C1, cells), F32),
            pltpu.VMEM((C1, cells), F32),
            pltpu.VMEM((C1, cells), BF16),
            pltpu.VMEM((C1, cells), BF16),
            pltpu.VMEM((28 * C1, small), BF16),
            pltpu.VMEM((9 * C2, small), BF16),
            pltpu.VMEM((GROWS, GY), F32),
            pltpu.VMEM((C1, GY), F32),
            pltpu.VMEM((n_lo, n_hi, per, GY), BF16),
            pltpu.VMEM((PZ * PX + 16, GY), BF16),
            pltpu.VMEM((n_lo - 1, n_hi, per, GY), BF16),
            pltpu.VMEM((n_hi, per, GY), BF16),
            pltpu.VMEM((n_hi, PZ * PX + 16, GY), BF16),
            pltpu.VMEM((2 * n_lo, PZ * PX, GY), BF16),
            pltpu.VMEM((n_lo - 1, 2, PZ * PX, GY), BF16),
            dma((n_lo - 1,)),
            dma((n_lo - 1,)),
            dma((n_lo - 1,)),
            dma((n_lo - 1,)),
            dma((across,)),
            dma((across,)),
            dma((n_hi - 1,)),
            dma((n_hi - 1,)),
            dma((n_lo - 1,)),
            dma((n_lo - 1,)),
        ],
        compiler_params=pltpu.CompilerParams(
            collective_id=1, has_side_effects=True, vmem_limit_bytes=32 * 2**20
        ),
        name="train",
    )(slot, patch, *weights)


def finish_kernel(heat_in, pred_in, grad_in, heat_out, pred_out, grad_out, done):
    copy = pltpu.make_async_copy(heat_in, heat_out, done)
    copy.start()
    total = grad_in[0].astype(F32)
    for t in range(1, grad_in.shape[0]):
        total = total + grad_in[t].astype(F32)
    grad_out[...] = total
    for s in range(2):
        for z in range(PZ):
            pred_out[s, z] = pred_in[s, z * PX : (z + 1) * PX, :].astype(BF16)
    copy.wait()


def finish(heat, preds, partials):
    return pl.pallas_call(
        finish_kernel,
        out_shape=(
            jax.ShapeDtypeStruct(heat.shape, F32),
            jax.ShapeDtypeStruct((2, PZ, PX, GY), BF16),
            jax.ShapeDtypeStruct(partials.shape[1:], F32),
        ),
        in_specs=[pl.BlockSpec(memory_space=pl.ANY), VMEM, VMEM],
        out_specs=(HBM, VMEM, VMEM),
        scratch_shapes=[pltpu.SemaphoreType.DMA],
        compiler_params=pltpu.CompilerParams(vmem_limit_bytes=8 * 2**20),
        name="finish",
    )(heat, preds, partials)


def local(
    n_sec,
    n_dp,
    heat_start,
    conductivity,
    patch_z,
    patch_x,
    slot_table,
    w_stem,
    w_lift,
    w_down,
    w_deep,
    w_merge,
    w_out,
):
    n_lo = LINE
    n_hi = n_dp // n_lo
    weights = (w_stem.T, w_lift, w_down.T, w_deep, w_merge, w_out)
    heat_two, patch, *ready = heat_steps(
        n_sec, n_dp, heat_start, conductivity, patch_z, patch_x, weights
    )
    scale = 1.0 / (n_sec * n_dp * PZ * PX * GY)
    preds, partials = train(scale, n_sec, n_hi, n_lo, slot_table, patch, ready)
    return finish(heat_two, preds, partials)


def solution(mesh):
    n_sec, n_dp = mesh.shape["section"], mesh.shape["dp"]
    both = ("section", "dp")
    return jax.shard_map(
        functools.partial(local, n_sec, n_dp),
        mesh=mesh,
        in_specs=(P(both, None, None), P(both, None, None), P(both), P(both), P(both)) + (P(),) * 6,
        out_specs=(P(both, None, None), P(both, None, None, None), P("dp", None)),
        check_vma=False,
    )
```

time: 53.5 us -> 40.6 us (0.76)
  Pallas kernels: 45.2 us -> 37.9 us
  local copies, waits for them, and re-layouts: 5.37 us -> 0 us
    pallas_call x2, Pallas kernels: 30.6 us -> 24.9 us  [the longest x1 23.5 us: train(): pl.pallas_call(functools.partial(train_kernel, scale, n_sec, n_hi, n_lo),...]
    unnamed x19 -> x0, local copies, waits for them, and re-layouts: 5.37 us -> none
    pallas_call x1, Pallas kernels: 14.7 us -> 13 us  [heat_steps(): pl.pallas_call(functools.partial(heat_kernel, n_sec, n_dp), out_shape=(ja...]
where the time goes in v2:
time: 40.6 us; the launch traced here: 40.5 us
  Pallas kernels  37.9 us (93%)
  between operations  2.59 us (6%)
    pallas_call x1, Pallas kernels, train(): pl.pallas_call(functools.partial(train_kernel, scale, n_sec, n_hi, n_lo),...  23.5 us
    pallas_call x1, Pallas kernels, heat_steps(): pl.pallas_call(functools.partial(heat_kernel, n_sec, n_dp), out_shape=(ja...  13 us
    pallas_call x1, Pallas kernels, finish(): pl.pallas_call(finish_kernel, out_shape=(jax.ShapeDtypeStruct(heat.shape,...  1.32 us

profile of v2, /device:TPU:1, one launch (start us, length us, event | category | flops | bytes accessed | tf_op | source)
XLA Modules:
  0.0 40.5 jit_solution(8538563534552651267)
XLA Ops:
  2.6 13.0 %heat.1 = (f32[16,32,128]{2,1,0:T(8,128)S(1)}, f32[3,4,8,128]{3,2,1,0:T(8,128)S(1)}, bf16[64,54]{1,0:T(8,128)(2,1)S(1)}, bf16[64,64]{1,0:T(8,128)(2,1)S(1)}, bf1...) custom-call(s32[1]{0:T(128)S(6)} %copy.14.pz_ref, ...), custom_call_target="tpu_custom_call" | custom-call | tf_op jit(solution)/shard_map/heat/pallas_call | solution.py:221
  15.6 23.5 %train.1 = (f32[2,32,128]{2,1,0:T(8,128)S(1)}, bf16[32,16,128]{2,1,0:T(8,128)(2,1)S(1)}) custom-call(s32[1]{0:T(128)S(6)} %copy.16.slot_ref, f32[3,4,8,128]{3,2,1,0:T(8,128)S(1)} %get-tuple-element.21.patch_ref, bf16[64,54]{1,0:T(8,128)(2,1)S(1)} %get-tuple-element.22.w_stem, bf16[64,64]{1,0:T(8,128)(2,1)S(1)} %get-tuple-element.23.w_lift, ...), custom_call_target="tpu_custom_call" | custom-call | tf_op jit(solution)/shard_map/train/pallas_call | solution.py:696
  39.2 1.3 %finish.1 = (f32[16,32,128]{2,1,0:T(8,128)}, bf16[2,4,8,128]{3,2,1,0:T(8,128)(2,1)}, f32[16,128]{1,0:T(8,128)}) custom-call(f32[16,32,128]{2,1,0:T(8,128)S(1)} %get-tuple-element.20.heat_in, f32[2,32,128]{2,1,0:T(8,128)S(1)} %get-tuple-element.35.pred_in, bf16[32,16,128]{2,1,0:T(8,128)(2,1)S(1)} %get-tuple-element.36.grad_in), custom_call_target="tpu_custom_call" | custom-call | tf_op jit(solution)/shard_map/finish/pallas_call | solution.py:756

commit v3 on v2

--- a/solution.py
+++ b/solution.py
@@ -40,6 +40,7 @@
     n_dp,
     pz_ref,
     px_ref,
+    slot_ref,
     u_hbm,
     k_hbm,
     stem_hbm,
@@ -61,8 +62,8 @@
     fine_t,
     coarse_ref,
     coarse_t,
-    proj_ref,
     proj_col,
+    slot_tile,
     v_stem,
     v_down,
     v_merge,
@@ -88,8 +89,16 @@
         return (lax.div(i, n_dp), lax.rem(i, n_dp))
 
     barrier = pltpu.get_barrier_semaphore()
-    for peer in (before, after):
-        pl.semaphore_signal(barrier, inc=1, device_id=place(peer), device_id_type=MESH)
+    below, above = me > 0, me < total - 1
+
+    @pl.when(below)
+    def _():
+        pl.semaphore_signal(barrier, inc=1, device_id=place(before), device_id_type=MESH)
+
+    @pl.when(above)
+    def _():
+        pl.semaphore_signal(barrier, inc=1, device_id=place(after), device_id_type=MESH)
+
     loads = [
         pltpu.make_async_copy(u_hbm, u_ref, load.at[0]),
         pltpu.make_async_copy(k_hbm, k_ref, load.at[1]),
@@ -102,16 +111,24 @@
     ]
     for copy in loads:
         copy.start()
-    pl.semaphore_wait(barrier, 2)
+    inner_slab = jnp.logical_and(below, above)
+
+    @pl.when(inner_slab)
+    def _():
+        pl.semaphore_wait(barrier, 2)
+
+    @pl.when(jnp.logical_not(inner_slab))
+    def _():
+        pl.semaphore_wait(barrier, 1)
+
     plan = (
         (u_hbm.at[pl.ds(depth - 2, 2)], ulo, after),
+        (k_hbm.at[pl.ds(depth - 2, 2)], klo, after),
         (u_hbm.at[pl.ds(0, 2)], uhi, before),
-        (k_hbm.at[pl.ds(depth - 2, 2)], klo, after),
         (k_hbm.at[pl.ds(0, 2)], khi, before),
     )
-    copies = []
-    for i, (src, dst, peer) in enumerate(plan):
-        copy = pltpu.make_async_remote_copy(
+    copies = [
+        pltpu.make_async_remote_copy(
             src_ref=src,
             dst_ref=dst,
             send_sem=send.at[i],
@@ -119,8 +136,29 @@
             device_id=place(peer),
             device_id_type=MESH,
         )
-        copy.start()
-        copies.append(copy)
+        for i, (src, dst, peer) in enumerate(plan)
+    ]
+    upward, downward = copies[0:2], copies[2:4]
+
+    @pl.when(above)
+    def _():
+        for copy in upward:
+            copy.start()
+
+    @pl.when(below)
+    def _():
+        for copy in downward:
+            copy.start()
+
+    @pl.when(me == 0)
+    def _():
+        ulo[...] = jnp.zeros_like(ulo)
+        klo[...] = jnp.zeros_like(klo)
+
+    @pl.when(me == total - 1)
+    def _():
+        uhi[...] = jnp.zeros_like(uhi)
+        khi[...] = jnp.zeros_like(khi)
 
     rows, lanes = u_ref.shape[1:]
     row = lax.broadcasted_iota(jnp.int32, (rows, lanes), 0)
@@ -167,7 +205,10 @@
     eye = unit[0:C1, 0:C1]
     unit = unit.astype(BF16)
     stem_ref[...] = mm(unit[0:C1, 0:C1], v_stem[...], NT).astype(BF16)
-    down_ref[...] = mm(unit, v_down[...], NT).astype(BF16)
+    for dy in range(3):
+        starts = [(j * 3 + dy) * C1 for j in range(9)]
+        part = jnp.concatenate([v_down[r : r + C1, :] for r in starts], axis=0)
+        down_ref[dy * C2 : (dy + 1) * C2, :] = mm(unit, part, NT).astype(BF16)
     for j in range(9):
         down_back[:, j * C2 : (j + 1) * C2] = v_down[j * 3 * C1 : (j + 1) * 3 * C1, :]
 
@@ -175,6 +216,7 @@
         return x.astype(F32).T.astype(BF16)
 
     lift_t[...] = turned(lift_ref[...])
+    slot_tile[...] = jnp.full((16, GY), slot_ref[0].astype(F32)).astype(BF16)
     deep_t[...] = turned(deep_ref[...])
     fine = v_merge[:, 0:C1]
     coarse = v_merge[:, C1 : C1 + C2]
@@ -183,18 +225,22 @@
     coarse_ref[...] = coarse
     coarse_t[...] = turned(coarse)
     row64 = v_proj[...].astype(F32)
-    proj_ref[...] = jnp.broadcast_to(row64, proj_ref.shape).astype(BF16)
     column = jnp.sum(jnp.where(eye, jnp.broadcast_to(row64, (C1, C1)), 0.0), axis=1, keepdims=True)
     proj_col[...] = jnp.broadcast_to(column, proj_col.shape)
 
-    for copy in copies:
-        copy.wait_recv()
+    @pl.when(below)
+    def _():
+        for copy in upward:
+            copy.wait_recv()
+
+    @pl.when(above)
+    def _():
+        for copy in downward:
+            copy.wait_recv()
+
     has_lo = (me > 0).astype(F32)
     has_hi = (me < total - 1).astype(F32)
-    ul = [ulo[0] * has_lo, ulo[1] * has_lo]
-    kl = [klo[0] * has_lo, klo[1] * has_lo]
-    uh = [uhi[0] * has_hi, uhi[1] * has_hi]
-    kh = [khi[0] * has_hi, khi[1] * has_hi]
+    ul, kl, uh, kh = ulo, klo, uhi, khi
     end = depth - 1
     h1[0] = has_lo * step(ul[0], ul[1], u_ref[0], kl[0], kl[1], k_ref[0])
     h1[1] = step(ul[1], u_ref[0], u_ref[1], kl[1], k_ref[0], k_ref[1])
@@ -211,12 +257,22 @@
         patch_ref[0, z] = h1[1 + pz + z, pl.ds(px, PX), :]
         patch_ref[1, z] = k_ref[pz + z, pl.ds(px, PX), :]
         patch_ref[2, z] = out_ref[pz + z, pl.ds(px, PX), :]
-    for copy in copies:
-        copy.wait_send()
-
-
-def heat_steps(n_sec, n_dp, heat, cond, patch_z, patch_x, weights):
+
+    @pl.when(above)
+    def _():
+        for copy in upward:
+            copy.wait_send()
+
+    @pl.when(below)
+    def _():
+        for copy in downward:
+            copy.wait_send()
+
+
+def heat_steps(n_sec, n_dp, heat, cond, patch_z, patch_x, slot, weights):
     layers = (2,) + heat.shape[1:]
+    operands = (heat, cond, *weights)
+    operands = [pltpu.with_memory_space_constraint(x, pltpu.HBM) for x in operands]
     taps = weights[0].shape[0]
     return pl.pallas_call(
         functools.partial(heat_kernel, n_sec, n_dp),
@@ -226,7 +282,7 @@
             jax.ShapeDtypeStruct((C1, taps), BF16),
             jax.ShapeDtypeStruct((C1, C1), BF16),
             jax.ShapeDtypeStruct((C1, C1), BF16),
-            jax.ShapeDtypeStruct((C2, 27 * C1), BF16),
+            jax.ShapeDtypeStruct((3 * C2, 9 * C1), BF16),
             jax.ShapeDtypeStruct((3 * C1, 9 * C2), BF16),
             jax.ShapeDtypeStruct((C2, C2), BF16),
             jax.ShapeDtypeStruct((C2, C2), BF16),
@@ -234,10 +290,10 @@
             jax.ShapeDtypeStruct((C1, C1), BF16),
             jax.ShapeDtypeStruct((C1, C2), BF16),
             jax.ShapeDtypeStruct((C2, C1), BF16),
-            jax.ShapeDtypeStruct((16, C1), BF16),
             jax.ShapeDtypeStruct((C1, GY), F32),
+            jax.ShapeDtypeStruct((16, GY), BF16),
         ),
-        in_specs=[SMEM, SMEM] + [HBM] * 8,
+        in_specs=[SMEM] * 3 + [HBM] * 8,
         out_specs=(VMEM,) * 15,
         scratch_shapes=[
             pltpu.VMEM(weights[0].shape, BF16),
@@ -259,7 +315,7 @@
             collective_id=0, has_side_effects=True, vmem_limit_bytes=16 * 2**20
         ),
         name="heat",
-    )(patch_z, patch_x, *[pltpu.with_memory_space_constraint(x, pltpu.HBM) for x in (heat, cond, *weights)])
+    )(patch_z, patch_x, slot, *operands)
 
 
 def silu_and_slope(z):
@@ -277,7 +333,7 @@
     n_sec,
     n_hi,
     n_lo,
-    slot_ref,
+    slot_tile,
     patch_ref,
     w_stem,
     w_lift,
@@ -290,7 +346,6 @@
     w_fine_t,
     w_coarse,
     w_coarse_t,
-    w_proj,
     w_proj_col,
     pred_out,
     buf2,
@@ -300,23 +355,28 @@
     l2,
     g1,
     g2,
-    merged_ref,
     dz_ref,
+    dz2_ref,
     colsd,
     colsz,
     pack,
     pair,
     grads,
     packet,
+    cbuf,
+    half_ref,
     buf1,
+    buf_late,
     acc,
     pbuf,
     q_ref,
     qbuf,
     s1,
     r1,
-    s1b,
-    r1b,
+    sc,
+    rc,
+    s5,
+    r5,
     s2,
     r2,
     s3,
@@ -330,10 +390,18 @@
     lo = lax.rem(dp, n_lo)
     across = n_sec * n_hi
     mine = sec * n_hi + hi
+    n_y = n_lo // 2
+    core = lax.rem(lo, 2)
+    other = 1 - core
+    y = lax.div(lo, 2)
 
     def in_line(d):
         peer = lax.rem(lo + d, n_lo)
         return peer, (sec, hi * n_lo + peer)
+
+    def in_y(d):
+        peer = lax.rem(y + d, n_y)
+        return peer, (sec, hi * n_lo + 2 * peer + core)
 
     def in_column(d):
         peer = lax.rem(mine + d, across)
@@ -388,7 +456,6 @@
         cols[:, b * GY : (b + 1) * GY] = tall[b * C1 : (b + 1) * C1, :].astype(BF16)
 
     taps = w_stem.shape[1]
-    depth = 27 * C1
     stem = w_stem[...]
     lift = w_lift[...]
     pooled = []
@@ -410,30 +477,33 @@
             pooled.append(rounded((block(both, 2 * xx) + block(both, 2 * xx + 1)) * 0.25))
 
     hz, hx = PZ // 2, PX // 2
-    shifted = []
-    for dy in range(3):
-        if dy == 0:
-            part = [jnp.where(lane64 == 0, 0.0, pltpu.roll(v, 1, 1)) for v in pooled]
-        elif dy == 1:
-            part = pooled
-        else:
-            part = [jnp.where(lane64 == GY - 1, 0.0, pltpu.roll(v, GY - 1, 1)) for v in pooled]
-        shifted.append([v.astype(BF16) for v in part])
     nothing = jnp.zeros((C1, GY), BF16)
+    pooled = [v.astype(BF16) for v in pooled]
     for dz in range(3):
         for dx in range(3):
-            for dy in range(3):
-                r = ((dz * 3 + dx) * 3 + dy) * C1
-                for z in range(hz):
-                    for x in range(hx):
-                        sz, sx = z + dz - 1, x + dx - 1
-                        inside = 0 <= sz < hz and 0 <= sx < hx
-                        b = z * hx + x
-                        colsd[r : r + C1, b * GY : (b + 1) * GY] = (
-                            shifted[dy][sz * hx + sx] if inside else nothing
-                        )
+            r = (dz * 3 + dx) * C1
+            for z in range(hz):
+                for x in range(hx):
+                    sz, sx = z + dz - 1, x + dx - 1
+                    inside = 0 <= sz < hz and 0 <= sx < hx
+                    b = z * hx + x
+                    colsd[r : r + C1, b * GY : (b + 1) * GY] = pooled[sz * hx + sx] if inside else nothing
+    depth = 9 * C1
     colsd[depth : depth + C1, :] = jnp.zeros((C1, small), BF16)
-    value, slope_down = silu_and_slope(mm(w_down[...], colsd[0:depth, :]))
+    products = mm(w_down[...], colsd[0:depth, :])
+    lane128 = lax.broadcasted_iota(jnp.int32, (C2, GY), 1)
+
+    def later(v):
+        return jnp.where(lane128 == 0, 0.0, pltpu.roll(v, 1, 1))
+
+    def sooner(v):
+        return jnp.where(lane128 == GY - 1, 0.0, pltpu.roll(v, GY - 1, 1))
+
+    summed = []
+    for b in range(hz * hx):
+        v = block(products, b)
+        summed.append(later(v[0:C2]) + v[C2 : 2 * C2] + sooner(v[2 * C2 : 3 * C2]))
+    value, slope_down = silu_and_slope(jnp.concatenate(summed, axis=1))
     coarse = value.astype(BF16)
     value, slope_deep = silu_and_slope(mm(w_deep[...], coarse))
     deeper = value.astype(BF16)
@@ -441,9 +511,8 @@
     lifted = mm(w_coarse[...], deeper)
 
     out_col = w_proj_col[...]
-    out8 = w_proj[0:8, :]
     fine_t = w_fine_t[...]
-    slim = []
+    d_out = jnp.zeros((C1, GY), F32)
     gathered = [None] * (hz * hx)
     forecast = []
     for z in range(PZ):
@@ -452,16 +521,15 @@
         added = [block(lifted, (z // 2) * hx + x // 2) for x in range(PX)]
         value, slope = silu_and_slope(mm(merge_fine, two) + jnp.concatenate(added, axis=1))
         merged = value.astype(BF16)
-        wide = mm(out8, merged)
+        held = merged.astype(F32)
         predicted = jnp.zeros((PX, GY), F32)
         for x in range(PX):
-            predicted = jnp.where(row8 == x, block(wide, x), predicted)
+            summed = jnp.sum(block(held, x) * out_col, axis=0, keepdims=True)
+            predicted = jnp.where(row8 == x, summed, predicted)
         forecast.append(predicted)
         misfit = (predicted - rounded(patch_ref[2, z])) * scale
-        d_wide = jnp.concatenate(
-            [jnp.broadcast_to(misfit[x : x + 1, :], (8, GY)) for x in range(PX)], axis=1
-        ).astype(BF16)
-        merged_ref[:, here] = merged
+        for x in range(PX):
+            d_out = d_out + block(held, x) * misfit[x : x + 1, :]
         d_merged = jnp.concatenate([out_col * misfit[x : x + 1, :] for x in range(PX)], axis=1)
         dz = rounded(d_merged) * slope
         for x in range(PX):
@@ -469,12 +537,11 @@
             gathered[b] = block(dz, x) if gathered[b] is None else gathered[b] + block(dz, x)
         dz = dz.astype(BF16)
         dz_ref[:, here] = dz
-        slim.append(d_wide)
 
     half = PZ * PX // 2
     packet[0:half, :] = jnp.concatenate(forecast[0 : PZ // 2], axis=0).astype(BF16)
     packet[half : 2 * half, :] = jnp.concatenate(forecast[PZ // 2 : PZ], axis=0).astype(BF16)
-    packet[2 * half : 2 * half + 16, :] = jnp.full((16, GY), slot_ref[0].astype(F32)).astype(BF16)
+    packet[2 * half : 2 * half + 16, :] = slot_tile[...]
     pl.semaphore_wait(barrier, n_lo - 1 + across - 1)
     packets = []
     for d in range(1, n_hi):
@@ -491,20 +558,38 @@
     r_ = lax.broadcasted_iota(jnp.int32, (C2, C2), 0)
     c_ = lax.broadcasted_iota(jnp.int32, (C2, C2), 1)
     parted = jnp.where(r_ < C1, 2 * r_, 2 * r_ - (C2 - 1)) == c_
-    dz_parted = mm(parted.astype(BF16), dz_down).astype(BF16)
+    dz_parted = mm(parted.astype(BF16), dz_down)
+    blocks = [block(dz_parted, b) for b in range(hz * hx)]
+    dz_shifts = jnp.concatenate(
+        [
+            jnp.concatenate([f(v) for v in blocks], axis=1).astype(BF16)
+            for f in (sooner, lambda v: v, later)
+        ],
+        axis=0,
+    )
+    d_down = mm(dz_shifts, colsd[...], NT)
+    low = lane64 < C1
+    turned_chunks = {}
+
+    def piece(h, lanes_low):
+        odd, h = divmod(h, 27)
+        zx, dy = divmod(h, 3)
+        q, high = divmod(zx, 2)
+        r = dy * C2 + odd * C1
+        chunk = d_down[r : r + C1, q * GY : (q + 1) * GY]
+        if bool(high) != lanes_low:
+            return chunk
+        if (r, q) not in turned_chunks:
+            turned_chunks[r, q] = pltpu.roll(chunk, C1, 1)
+        return turned_chunks[r, q]
+
     base = 27 + 32
-    chunks = [mm(dz_parted, colsd[j * C2 : (j + 1) * C2, :], NT) for j in range(14)]
-    low = lane64 < C1
-    for j in range(13):
-        pack[pl.ds(base + j, C1, stride=27), :] = chunks[j][0:C1]
-        pack[pl.ds(base + 14 + j, C1, stride=27), :] = pltpu.roll(
-            jnp.where(low, chunks[j + 1][C1:C2], chunks[j][C1:C2]), C1, 1
+    for j in range(27):
+        pack[pl.ds(base + j, C1, stride=27), :] = jnp.where(
+            low, piece(2 * j, True), piece(2 * j + 1, False)
         )
-    pack[pl.ds(base + 13, C1, stride=27), :] = jnp.where(
-        low, chunks[13][0:C1], pltpu.roll(chunks[0][C1:C2], C1, 1)
-    )
-
-    per = grads.shape[2]
+
+    per = grads.shape[3]
     first = -(-(27 + 32) // (per * n_lo))
     top = n_hi - (27 + 32 + 27 * C1) // (per * n_lo)
     tail = first + top
@@ -512,33 +597,51 @@
     def emit(hi_):
         for lo_ in range(n_lo):
             start = (hi_ * n_lo + lo_) * per
-            grads[lo_, (hi_ + top) % n_hi] = pack[start : start + per, :].astype(BF16)
+            grads[lo_ % 2, lo_ // 2, (hi_ + top) % n_hi] = pack[start : start + per, :].astype(BF16)
 
     for h in range(first, n_hi - top):
         emit(h)
-    early = []
-    for d in range(1, n_lo):
-        peer, device = in_line(d)
-        early.append(
-            send(
-                grads.at[peer, pl.ds(tail, n_hi - tail)],
-                buf1.at[d - 1, pl.ds(tail, n_hi - tail)],
-                s1.at[d - 1],
-                r1.at[d - 1],
-                device,
+
+    def swap(begin, count, i):
+        return send(
+            grads.at[other, :, pl.ds(begin, count)],
+            cbuf.at[:, pl.ds(begin, count)],
+            sc.at[i],
+            rc.at[i],
+            (sec, hi * n_lo + 2 * y + other),
+        )
+
+    def chip_sum(begin, count, copy, i):
+        copy.wait_recv()
+        part = slice(begin, begin + count)
+        for y_ in range(n_y):
+            total = grads[core, y_, part].astype(F32) + cbuf[y_, part].astype(F32)
+            half_ref[y_, part] = total.astype(BF16)
+        copies = []
+        for d in range(1, n_y):
+            peer, device = in_y(d)
+            copies.append(
+                send(
+                    half_ref.at[peer, pl.ds(begin, count)],
+                    buf1.at[d - 1, pl.ds(begin, count)],
+                    s1.at[i, d - 1],
+                    r1.at[i, d - 1],
+                    device,
+                )
             )
-        )
+        return copies
+
+    swap_down = swap(tail, n_hi - tail, 0)
+
+    def twice(x):
+        pair[:, 0:C1] = x
+        pair[:, C1:GY] = jnp.zeros((C1, GY - C1), F32)
+        once = pair[...]
+        return once + pltpu.roll(once, C1, 1)
 
     d_coarse_merge = mm(d_lifted, deeper, NT)
     d_deep = mm(dz_deep, coarse, NT)
-    d_fine = jnp.zeros((C1, GY), F32)
-    d_out = jnp.zeros((8, GY), F32)
-    for z in range(PZ):
-        here = slice(z * plane, (z + 1) * plane)
-        merged = merged_ref[:, here]
-        d_out = d_out + mm(slim[z], jnp.concatenate([merged, merged], axis=0), NT)
-        two = l2[:, here]
-        d_fine = d_fine + mm(dz_ref[:, here], jnp.concatenate([two, two], axis=0), NT)
+    d_fine = twice(mm(dz_ref[...], l2[...], NT))
     low32 = lax.broadcasted_iota(jnp.int32, (32, GY), 1) < C1
     base = 27 + 32 + 27 * C1
     pack[base : base + C2, :] = d_deep
@@ -552,9 +655,17 @@
     pack[pl.ds(base + 1, 32, stride=3), :] = jnp.where(low32, turn, fine_even_odd[1])
     pack[pl.ds(base + 2, 32, stride=3), :] = coarse_even_odd[1]
     base = base + 96
-    pack[base : base + 1, :] = jnp.where(lane8[0:1] < C1, d_out[0:1, :], 0.0)
+    column = jnp.sum(d_out, axis=1, keepdims=True)
+    across_ = lane64 == lax.broadcasted_iota(jnp.int32, (C1, GY), 0)
+    pack[base : base + 1, :] = jnp.sum(
+        jnp.where(across_, jnp.broadcast_to(column, (C1, GY)), 0.0), axis=0, keepdims=True
+    )
     pack[base + 1 : GROWS, :] = jnp.zeros((GROWS - base - 1, GY), F32)
 
+
+    for h in range(n_hi - top, n_hi):
+        emit(h)
+    swap_join = swap(0, top, 1)
 
     blank = jnp.zeros((C2, GY), BF16)
     for dz in range(3):
@@ -568,6 +679,7 @@
                     colsz[j * C2 : (j + 1) * C2, b * GY : (b + 1) * GY] = (
                         block(dz_down, sz * hx + sx) if inside else blank
                     )
+    early = chip_sum(tail, n_hi - tail, swap_down, 0)
     d_shifted = mm(wback[...], colsz[...])
     d_pooled = []
     for b in range(hz * hx):
@@ -577,18 +689,19 @@
         total = total + jnp.where(lane64 == 0, 0.0, pltpu.roll(whole[2 * C1 : 3 * C1], 1, 1))
         d_pooled.append(rounded(total) * 0.25)
 
+    early += chip_sum(0, top, swap_join, 1)
     lift_t = w_lift_t[...]
-    d_lift = jnp.zeros((C1, GY), F32)
     d_stem = jnp.zeros((C1, C1), F32)
     for z in range(PZ):
         here = slice(z * plane, (z + 1) * plane)
         spread = jnp.concatenate([d_pooled[(z // 2) * hx + x // 2] for x in range(PX)], axis=1)
         dz = ((rounded(mm(fine_t, dz_ref[:, here])) + spread) * g2[:, here]).astype(BF16)
-        one = l1[:, here]
-        d_lift = d_lift + mm(dz, jnp.concatenate([one, one], axis=0), NT)
+        dz2_ref[:, here] = dz
         d_one = rounded(mm(lift_t, dz))
         dz = (d_one * g1[:, here]).astype(BF16)
         d_stem = d_stem + mm(dz, cols[:, here], NT)
+
+    d_lift = twice(mm(dz2_ref[...], l1[...], NT))
 
     pair[:, 0:C1] = d_stem
     pair[:, C1:GY] = jnp.zeros((C1, GY - C1), F32)
@@ -612,17 +725,17 @@
     pack[27 : 27 + 32, :] = jnp.where(low32, pair[pl.ds(0, 32, stride=2), :], pair[pl.ds(1, 32, stride=2), :])
 
 
-    for h in list(range(first)) + list(range(n_hi - top, n_hi)):
+    for h in range(first):
         emit(h)
     late = []
     for d in range(1, n_lo):
         peer, device = in_line(d)
         late.append(
             send(
-                grads.at[peer, pl.ds(0, tail)],
-                buf1.at[d - 1, pl.ds(0, tail)],
-                s1b.at[d - 1],
-                r1b.at[d - 1],
+                grads.at[lax.rem(peer, 2), lax.div(peer, 2), pl.ds(top, first)],
+                buf_late.at[d - 1],
+                s5.at[d - 1],
+                r5.at[d - 1],
                 device,
             )
         )
@@ -647,17 +760,26 @@
         peer, device = in_line(d)
         routed.append(send(q_ref.at[pl.ds(2 * peer, 2)], qbuf.at[d - 1], s4.at[d - 1], r4.at[d - 1], device))
 
-    for copy in early + late:
+    for copy in early:
         copy.wait_recv()
-
-    partials = []
-    for e in range(1, n_hi + 1):
-        h = lax.rem(hi + e, n_hi)
-        at = lax.rem(h + top, n_hi)
-        value = grads[lo, at].astype(F32)
-        for d in range(n_lo - 1):
+    for h in range(first, n_hi):
+        at = (h + top) % n_hi
+        value = half_ref[y, at].astype(F32)
+        for d in range(n_y - 1):
             value = value + buf1[d, at].astype(F32)
         acc[h] = value.astype(BF16)
+    for copy in late:
+        copy.wait_recv()
+    for h in range(first):
+        value = grads[core, y, h + top].astype(F32)
+        for d in range(n_lo - 1):
+            value = value + buf_late[d, h].astype(F32)
+        acc[h] = value.astype(BF16)
+    partials = []
+    ring = 8
+    far_first = sorted(range(1, n_hi + 1), key=lambda e: (e == n_hi, -min(e % ring, ring - e % ring)))
+    for e in far_first:
+        h = lax.rem(hi + e, n_hi)
         for q in range(n_sec):
             if e == n_hi and q == 0:
                 buf2[mine] = acc[h]
@@ -683,7 +805,7 @@
 
     for copy in partials:
         copy.wait_recv()
-    for copy in packets + early + late + routed + partials:
+    for copy in [swap_down, swap_join] + packets + early + late + routed + partials:
         copy.wait_send()
 
 
@@ -692,6 +814,8 @@
     small = cells // 4
     per = GROWS // (n_lo * n_hi)
     across = n_sec * n_hi
+    n_y = n_lo // 2
+    first = -(-(27 + 32) // (per * n_lo))
     dma = pltpu.SemaphoreType.DMA
     return pl.pallas_call(
         functools.partial(train_kernel, scale, n_sec, n_hi, n_lo),
@@ -699,7 +823,7 @@
             jax.ShapeDtypeStruct((2, PZ * PX, GY), F32),
             jax.ShapeDtypeStruct((across, per, GY), BF16),
         ),
-        in_specs=[SMEM] + [VMEM] * 14,
+        in_specs=[VMEM] * 14,
         out_specs=(VMEM, VMEM),
         scratch_shapes=[
             pltpu.VMEM((PZ * PX * C1, GY), F32),
@@ -710,19 +834,24 @@
             pltpu.VMEM((C1, cells), F32),
             pltpu.VMEM((C1, cells), BF16),
             pltpu.VMEM((C1, cells), BF16),
-            pltpu.VMEM((28 * C1, small), BF16),
+            pltpu.VMEM((10 * C1, small), BF16),
             pltpu.VMEM((9 * C2, small), BF16),
             pltpu.VMEM((GROWS, GY), F32),
             pltpu.VMEM((C1, GY), F32),
-            pltpu.VMEM((n_lo, n_hi, per, GY), BF16),
+            pltpu.VMEM((2, n_y, n_hi, per, GY), BF16),
             pltpu.VMEM((PZ * PX + 16, GY), BF16),
-            pltpu.VMEM((n_lo - 1, n_hi, per, GY), BF16),
+            pltpu.VMEM((n_y, n_hi, per, GY), BF16),
+            pltpu.VMEM((n_y, n_hi, per, GY), BF16),
+            pltpu.VMEM((n_y - 1, n_hi, per, GY), BF16),
+            pltpu.VMEM((n_lo - 1, first, per, GY), BF16),
             pltpu.VMEM((n_hi, per, GY), BF16),
             pltpu.VMEM((n_hi, PZ * PX + 16, GY), BF16),
             pltpu.VMEM((2 * n_lo, PZ * PX, GY), BF16),
             pltpu.VMEM((n_lo - 1, 2, PZ * PX, GY), BF16),
-            dma((n_lo - 1,)),
-            dma((n_lo - 1,)),
+            dma((2, n_y - 1)),
+            dma((2, n_y - 1)),
+            dma((2,)),
+            dma((2,)),
             dma((n_lo - 1,)),
             dma((n_lo - 1,)),
             dma((across,)),
@@ -786,11 +915,11 @@
     n_lo = LINE
     n_hi = n_dp // n_lo
     weights = (w_stem.T, w_lift, w_down.T, w_deep, w_merge, w_out)
-    heat_two, patch, *ready = heat_steps(
-        n_sec, n_dp, heat_start, conductivity, patch_z, patch_x, weights
+    heat_two, patch, *ready, slot = heat_steps(
+        n_sec, n_dp, heat_start, conductivity, patch_z, patch_x, slot_table, weights
     )
     scale = 1.0 / (n_sec * n_dp * PZ * PX * GY)
-    preds, partials = train(scale, n_sec, n_hi, n_lo, slot_table, patch, ready)
+    preds, partials = train(scale, n_sec, n_hi, n_lo, slot, patch, ready)
     return finish(heat_two, preds, partials)
 
 

time: 40.6 us -> 40 us (0.985)
  Pallas kernels: 37.9 us -> 37.3 us
    pallas_call x1, Pallas kernels: 13 us -> 5.55 us  [heat_steps(): pl.pallas_call(functools.partial(heat_kernel, n_sec, n_dp), out_shape=(ja...]
    pallas_call x1, Pallas kernels: 23.5 us -> 30.4 us  [train(): pl.pallas_call(functools.partial(train_kernel, scale, n_sec, n_hi, n_lo),...]
where the time goes in v3:
time: 40 us; the launch traced here: 39.9 us
  Pallas kernels  37.3 us (93%)
  between operations  2.59 us (6%)
    pallas_call x1, Pallas kernels, train(): pl.pallas_call(functools.partial(train_kernel, scale, n_sec, n_hi, n_lo),...  30.4 us
    pallas_call x1, Pallas kernels, heat_steps(): pl.pallas_call(functools.partial(heat_kernel, n_sec, n_dp), out_shape=(ja...  5.55 us
    pallas_call x1, Pallas kernels, finish(): pl.pallas_call(finish_kernel, out_shape=(jax.ShapeDtypeStruct(heat.shape,...  1.32 us

profile of v3, /device:TPU:1, one launch (start us, length us, event | category | flops | bytes accessed | tf_op | source)
XLA Modules:
  0.0 39.9 jit_solution(15026541525750283756)
XLA Ops:
  2.6 5.6 %heat.1 = (f32[16,32,128]{2,1,0:T(8,128)S(1)}, f32[3,4,8,128]{3,2,1,0:T(8,128)S(1)}, bf16[64,54]{1,0:T(8,128)(2,1)S(1)}, bf16[64,64]{1,0:T(8,128)(2,1)S(1)}, bf1...) custom-call(s32[1]{0:T(128)S(6)} %copy.14.pz_ref, ...), custom_call_target="tpu_custom_call" | custom-call | tf_op jit(solution)/shard_map/heat/pallas_call | solution.py:277
  8.1 30.4 %train.1 = (f32[2,32,128]{2,1,0:T(8,128)S(1)}, bf16[32,16,128]{2,1,0:T(8,128)(2,1)S(1)}) custom-call(bf16[16,128]{1,0:T(8,128)(2,1)S(1)} %get-tuple-element.21.slot_tile, f32[3,4,8,128]{3,2,1,0:T(8,128)S(1)} %get-tuple-element.22.patch_ref, bf16[64,54]{1,0:T(8,128)(2,1)S(1)} %get-tuple-element.23.w_stem, bf16[64,64]{1,0:T(8,128)(2,1)S(1)} %get-tuple-element.24.w_lift, ...), custom_call_target="tpu_custom_call" | custom-call | tf_op jit(solution)/shard_map/train/pallas_call | solution.py:820
  38.6 1.3 %finish.1 = (f32[16,32,128]{2,1,0:T(8,128)}, bf16[2,4,8,128]{3,2,1,0:T(8,128)(2,1)}, f32[16,128]{1,0:T(8,128)}) custom-call(f32[16,32,128]{2,1,0:T(8,128)S(1)} %get-tuple-element.20.heat_in, f32[2,32,128]{2,1,0:T(8,128)S(1)} %get-tuple-element.35.pred_in, bf16[32,16,128]{2,1,0:T(8,128)(2,1)S(1)} %get-tuple-element.36.grad_in), custom_call_target="tpu_custom_call" | custom-call | tf_op jit(solution)/shard_map/finish/pallas_call | solution.py:885

commit v4 on v3

--- a/solution.py
+++ b/solution.py
@@ -740,26 +740,6 @@
             )
         )
 
-    for copy in packets:
-        copy.wait_recv()
-    rows = PZ * PX
-
-    def route(q, carry):
-        wanted = (hi * (2 * n_lo) + q).astype(F32)
-        value = jnp.zeros((rows, GY), F32)
-        for src in range(n_hi):
-            named = pbuf[src, rows : rows + 16, :].astype(F32)
-            named = jnp.concatenate([named] * (rows // 16), axis=0)
-            value = value + jnp.where(named == wanted, pbuf[src, 0:rows, :].astype(F32), 0.0)
-        q_ref[q] = value.astype(BF16)
-        return carry
-
-    lax.fori_loop(0, 2 * n_lo, route, 0)
-    routed = []
-    for d in range(1, n_lo):
-        peer, device = in_line(d)
-        routed.append(send(q_ref.at[pl.ds(2 * peer, 2)], qbuf.at[d - 1], s4.at[d - 1], r4.at[d - 1], device))
-
     for copy in early:
         copy.wait_recv()
     for h in range(first, n_hi):
@@ -794,6 +774,26 @@
                     (owner, h * n_lo + lo),
                 )
             )
+
+    for copy in packets:
+        copy.wait_recv()
+    rows = PZ * PX
+
+    def route(q, carry):
+        wanted = (hi * (2 * n_lo) + q).astype(F32)
+        value = jnp.zeros((rows, GY), F32)
+        for src in range(n_hi):
+            named = pbuf[src, rows : rows + 16, :].astype(F32)
+            named = jnp.concatenate([named] * (rows // 16), axis=0)
+            value = value + jnp.where(named == wanted, pbuf[src, 0:rows, :].astype(F32), 0.0)
+        q_ref[q] = value.astype(BF16)
+        return carry
+
+    lax.fori_loop(0, 2 * n_lo, route, 0)
+    routed = []
+    for d in range(1, n_lo):
+        peer, device = in_line(d)
+        routed.append(send(q_ref.at[pl.ds(2 * peer, 2)], qbuf.at[d - 1], s4.at[d - 1], r4.at[d - 1], device))
 
     for copy in routed:
         copy.wait_recv()

time: 40 us -> 39.9 us (level)
  no operation moved by 1% of the time
where the time goes in v4:
time: 39.9 us; the launch traced here: 39.8 us
  Pallas kernels  37.2 us (93%)
  between operations  2.59 us (6%)
    pallas_call x1, Pallas kernels, train(): pl.pallas_call(functools.partial(train_kernel, scale, n_sec, n_hi, n_lo),...  30.3 us
    pallas_call x1, Pallas kernels, heat_steps(): pl.pallas_call(functools.partial(heat_kernel, n_sec, n_dp), out_shape=(ja...  5.55 us
    pallas_call x1, Pallas kernels, finish(): pl.pallas_call(finish_kernel, out_shape=(jax.ShapeDtypeStruct(heat.shape,...  1.32 us

profile of v4, /device:TPU:1, one launch (start us, length us, event | category | flops | bytes accessed | tf_op | source)
XLA Modules:
  0.0 39.8 jit_solution(4063603589397503203)
XLA Ops:
  2.6 5.6 %heat.1 = (f32[16,32,128]{2,1,0:T(8,128)S(1)}, f32[3,4,8,128]{3,2,1,0:T(8,128)S(1)}, bf16[64,54]{1,0:T(8,128)(2,1)S(1)}, bf16[64,64]{1,0:T(8,128)(2,1)S(1)}, bf1...) custom-call(s32[1]{0:T(128)S(6)} %copy.14.pz_ref, ...), custom_call_target="tpu_custom_call" | custom-call | tf_op jit(solution)/shard_map/heat/pallas_call | solution.py:277
  8.1 30.3 %train.1 = (f32[2,32,128]{2,1,0:T(8,128)S(1)}, bf16[32,16,128]{2,1,0:T(8,128)(2,1)S(1)}) custom-call(bf16[16,128]{1,0:T(8,128)(2,1)S(1)} %get-tuple-element.21.slot_tile, f32[3,4,8,128]{3,2,1,0:T(8,128)S(1)} %get-tuple-element.22.patch_ref, bf16[64,54]{1,0:T(8,128)(2,1)S(1)} %get-tuple-element.23.w_stem, bf16[64,64]{1,0:T(8,128)(2,1)S(1)} %get-tuple-element.24.w_lift, ...), custom_call_target="tpu_custom_call" | custom-call | tf_op jit(solution)/shard_map/train/pallas_call | solution.py:820
  38.5 1.3 %finish.1 = (f32[16,32,128]{2,1,0:T(8,128)}, bf16[2,4,8,128]{3,2,1,0:T(8,128)(2,1)}, f32[16,128]{1,0:T(8,128)}) custom-call(f32[16,32,128]{2,1,0:T(8,128)S(1)} %get-tuple-element.20.heat_in, f32[2,32,128]{2,1,0:T(8,128)S(1)} %get-tuple-element.35.pred_in, bf16[32,16,128]{2,1,0:T(8,128)(2,1)S(1)} %get-tuple-element.36.grad_in), custom_call_target="tpu_custom_call" | custom-call | tf_op jit(solution)/shard_map/finish/pallas_call | solution.py:885

commit v5 on v4

--- a/solution.py
+++ b/solution.py
@@ -418,6 +418,11 @@
         copy.start()
         return copy
 
+    def group(like, ssem, rsem, device):
+        return pltpu.make_async_remote_copy(
+            src_ref=like, dst_ref=like, send_sem=ssem, recv_sem=rsem, device_id=device, device_id_type=MESH
+        )
+
     barrier = pltpu.get_barrier_semaphore()
     for d in range(1, across):
         pl.semaphore_signal(barrier, inc=1, device_id=in_column(d)[1], device_id_type=MESH)
@@ -543,10 +548,10 @@
     packet[half : 2 * half, :] = jnp.concatenate(forecast[PZ // 2 : PZ], axis=0).astype(BF16)
     packet[2 * half : 2 * half + 16, :] = slot_tile[...]
     pl.semaphore_wait(barrier, n_lo - 1 + across - 1)
-    packets = []
     for d in range(1, n_hi):
         peer, device = in_part(d)
-        packets.append(send(packet, pbuf.at[d], s3.at[d - 1], r3.at[d - 1], device))
+        send(packet, pbuf.at[d], s3, r3, device)
+    packets = group(pbuf.at[pl.ds(1, n_hi - 1)], s3, r3, device)
     pbuf[0] = packet[...]
 
     d_lifted = jnp.concatenate(gathered, axis=1).astype(BF16)
@@ -617,19 +622,16 @@
         for y_ in range(n_y):
             total = grads[core, y_, part].astype(F32) + cbuf[y_, part].astype(F32)
             half_ref[y_, part] = total.astype(BF16)
-        copies = []
         for d in range(1, n_y):
             peer, device = in_y(d)
-            copies.append(
-                send(
-                    half_ref.at[peer, pl.ds(begin, count)],
-                    buf1.at[d - 1, pl.ds(begin, count)],
-                    s1.at[i, d - 1],
-                    r1.at[i, d - 1],
-                    device,
-                )
+            send(
+                half_ref.at[peer, pl.ds(begin, count)],
+                buf1.at[d - 1, pl.ds(begin, count)],
+                s1.at[i],
+                r1.at[i],
+                device,
             )
-        return copies
+        return group(buf1.at[:, pl.ds(begin, count)], s1.at[i], r1.at[i], device)
 
     swap_down = swap(tail, n_hi - tail, 0)
 
@@ -679,7 +681,7 @@
                     colsz[j * C2 : (j + 1) * C2, b * GY : (b + 1) * GY] = (
                         block(dz_down, sz * hx + sx) if inside else blank
                     )
-    early = chip_sum(tail, n_hi - tail, swap_down, 0)
+    early_down = chip_sum(tail, n_hi - tail, swap_down, 0)
     d_shifted = mm(wback[...], colsz[...])
     d_pooled = []
     for b in range(hz * hx):
@@ -689,7 +691,7 @@
         total = total + jnp.where(lane64 == 0, 0.0, pltpu.roll(whole[2 * C1 : 3 * C1], 1, 1))
         d_pooled.append(rounded(total) * 0.25)
 
-    early += chip_sum(0, top, swap_join, 1)
+    early_join = chip_sum(0, top, swap_join, 1)
     lift_t = w_lift_t[...]
     d_stem = jnp.zeros((C1, C1), F32)
     for z in range(PZ):
@@ -727,20 +729,18 @@
 
     for h in range(first):
         emit(h)
-    late = []
     for d in range(1, n_lo):
         peer, device = in_line(d)
-        late.append(
-            send(
-                grads.at[lax.rem(peer, 2), lax.div(peer, 2), pl.ds(top, first)],
-                buf_late.at[d - 1],
-                s5.at[d - 1],
-                r5.at[d - 1],
-                device,
-            )
+        send(
+            grads.at[lax.rem(peer, 2), lax.div(peer, 2), pl.ds(top, first)],
+            buf_late.at[d - 1],
+            s5,
+            r5,
+            device,
         )
-
-    for copy in early:
+    late = group(buf_late, s5, r5, device)
+
+    for copy in (early_down, early_join):
         copy.wait_recv()
     for h in range(first, n_hi):
         at = (h + top) % n_hi
@@ -748,14 +748,12 @@
         for d in range(n_y - 1):
             value = value + buf1[d, at].astype(F32)
         acc[h] = value.astype(BF16)
-    for copy in late:
-        copy.wait_recv()
+    late.wait_recv()
     for h in range(first):
         value = grads[core, y, h + top].astype(F32)
         for d in range(n_lo - 1):
             value = value + buf_late[d, h].astype(F32)
         acc[h] = value.astype(BF16)
-    partials = []
     ring = 8
     far_first = sorted(range(1, n_hi + 1), key=lambda e: (e == n_hi, -min(e % ring, ring - e % ring)))
     for e in far_first:
@@ -765,18 +763,11 @@
                 buf2[mine] = acc[h]
                 continue
             owner = lax.rem(sec + q, n_sec)
-            partials.append(
-                send(
-                    acc.at[h],
-                    buf2.at[mine],
-                    s2.at[q * n_hi + e - 1],
-                    r2.at[q * n_hi + e - 1],
-                    (owner, h * n_lo + lo),
-                )
-            )
-
-    for copy in packets:
-        copy.wait_recv()
+            device = (owner, h * n_lo + lo)
+            send(acc.at[h], buf2.at[mine], s2, r2, device)
+    partials = group(buf2.at[pl.ds(0, across - 1)], s2, r2, device)
+
+    packets.wait_recv()
     rows = PZ * PX
 
     def route(q, carry):
@@ -790,22 +781,20 @@
         return carry
 
     lax.fori_loop(0, 2 * n_lo, route, 0)
-    routed = []
     for d in range(1, n_lo):
         peer, device = in_line(d)
-        routed.append(send(q_ref.at[pl.ds(2 * peer, 2)], qbuf.at[d - 1], s4.at[d - 1], r4.at[d - 1], device))
-
-    for copy in routed:
-        copy.wait_recv()
+        send(q_ref.at[pl.ds(2 * peer, 2)], qbuf.at[d - 1], s4, r4, device)
+    routed = group(qbuf, s4, r4, device)
+
+    routed.wait_recv()
     for s in range(2):
         value = q_ref[2 * lo + s].astype(F32)
         for d in range(n_lo - 1):
             value = value + qbuf[d, s].astype(F32)
         pred_out[s] = value
 
-    for copy in partials:
-        copy.wait_recv()
-    for copy in [swap_down, swap_join] + packets + early + late + routed + partials:
+    partials.wait_recv()
+    for copy in (swap_down, swap_join, packets, early_down, early_join, late, routed, partials):
         copy.wait_send()
 
 
@@ -848,18 +837,18 @@
             pltpu.VMEM((n_hi, PZ * PX + 16, GY), BF16),
             pltpu.VMEM((2 * n_lo, PZ * PX, GY), BF16),
             pltpu.VMEM((n_lo - 1, 2, PZ * PX, GY), BF16),
-            dma((2, n_y - 1)),
-            dma((2, n_y - 1)),
             dma((2,)),
             dma((2,)),
-            dma((n_lo - 1,)),
-            dma((n_lo - 1,)),
-            dma((across,)),
-            dma((across,)),
-            dma((n_hi - 1,)),
-            dma((n_hi - 1,)),
-            dma((n_lo - 1,)),
-            dma((n_lo - 1,)),
+            dma((2,)),
+            dma((2,)),
+            dma,
+            dma,
+            dma,
+            dma,
+            dma,
+            dma,
+            dma,
+            dma,
         ],
         compiler_params=pltpu.CompilerParams(
             collective_id=1, has_side_effects=True, vmem_limit_bytes=32 * 2**20

time: 39.9 us -> 38.7 us (0.970)
  Pallas kernels: 37.2 us -> 36 us
    pallas_call x1, Pallas kernels: 30.3 us -> 29.1 us  [train(): pl.pallas_call(functools.partial(train_kernel, scale, n_sec, n_hi, n_lo),...]
where the time goes in v5:
time: 38.7 us; the launch traced here: 38.6 us
  Pallas kernels  36 us (93%)
  between operations  2.59 us (7%)
    pallas_call x1, Pallas kernels, train(): pl.pallas_call(functools.partial(train_kernel, scale, n_sec, n_hi, n_lo),...  29.1 us
    pallas_call x1, Pallas kernels, heat_steps(): pl.pallas_call(functools.partial(heat_kernel, n_sec, n_dp), out_shape=(ja...  5.55 us
    pallas_call x1, Pallas kernels, finish(): pl.pallas_call(finish_kernel, out_shape=(jax.ShapeDtypeStruct(heat.shape,...  1.32 us

profile of v5, /device:TPU:1, one launch (start us, length us, event | category | flops | bytes accessed | tf_op | source)
XLA Modules:
  0.0 38.6 jit_solution(3205648547686926622)
XLA Ops:
  2.6 5.6 %heat.1 = (f32[16,32,128]{2,1,0:T(8,128)S(1)}, f32[3,4,8,128]{3,2,1,0:T(8,128)S(1)}, bf16[64,54]{1,0:T(8,128)(2,1)S(1)}, bf16[64,64]{1,0:T(8,128)(2,1)S(1)}, bf1...) custom-call(s32[1]{0:T(128)S(6)} %copy.14.pz_ref, ...), custom_call_target="tpu_custom_call" | custom-call | tf_op jit(solution)/shard_map/heat/pallas_call | solution.py:277
  8.1 29.1 %train.1 = (f32[2,32,128]{2,1,0:T(8,128)S(1)}, bf16[32,16,128]{2,1,0:T(8,128)(2,1)S(1)}) custom-call(bf16[16,128]{1,0:T(8,128)(2,1)S(1)} %get-tuple-element.21.slot_tile, f32[3,4,8,128]{3,2,1,0:T(8,128)S(1)} %get-tuple-element.22.patch_ref, bf16[64,54]{1,0:T(8,128)(2,1)S(1)} %get-tuple-element.23.w_stem, bf16[64,64]{1,0:T(8,128)(2,1)S(1)} %get-tuple-element.24.w_lift, ...), custom_call_target="tpu_custom_call" | custom-call | tf_op jit(solution)/shard_map/train/pallas_call | solution.py:809
  37.3 1.3 %finish.1 = (f32[16,32,128]{2,1,0:T(8,128)}, bf16[2,4,8,128]{3,2,1,0:T(8,128)(2,1)}, f32[16,128]{1,0:T(8,128)}) custom-call(f32[16,32,128]{2,1,0:T(8,128)S(1)} %get-tuple-element.20.heat_in, f32[2,32,128]{2,1,0:T(8,128)S(1)} %get-tuple-element.35.pred_in, bf16[32,16,128]{2,1,0:T(8,128)(2,1)S(1)} %get-tuple-element.36.grad_in), custom_call_target="tpu_custom_call" | custom-call | tf_op jit(solution)/shard_map/finish/pallas_call | solution.py:874

commit v6 on v5

--- a/solution.py
+++ b/solution.py
@@ -35,7 +35,9 @@
     return lax.dot_general(a, b, dims, preferred_element_type=F32)
 
 
-def heat_kernel(
+def heat_part(
+    enter,
+    ready,
     n_sec,
     n_dp,
     pz_ref,
@@ -88,17 +90,8 @@
     def place(i):
         return (lax.div(i, n_dp), lax.rem(i, n_dp))
 
-    barrier = pltpu.get_barrier_semaphore()
     below, above = me > 0, me < total - 1
-
-    @pl.when(below)
-    def _():
-        pl.semaphore_signal(barrier, inc=1, device_id=place(before), device_id_type=MESH)
-
-    @pl.when(above)
-    def _():
-        pl.semaphore_signal(barrier, inc=1, device_id=place(after), device_id_type=MESH)
-
+    enter()
     loads = [
         pltpu.make_async_copy(u_hbm, u_ref, load.at[0]),
         pltpu.make_async_copy(k_hbm, k_ref, load.at[1]),
@@ -111,16 +104,7 @@
     ]
     for copy in loads:
         copy.start()
-    inner_slab = jnp.logical_and(below, above)
-
-    @pl.when(inner_slab)
-    def _():
-        pl.semaphore_wait(barrier, 2)
-
-    @pl.when(jnp.logical_not(inner_slab))
-    def _():
-        pl.semaphore_wait(barrier, 1)
-
+    ready()
     plan = (
         (u_hbm.at[pl.ds(depth - 2, 2)], ulo, after),
         (k_hbm.at[pl.ds(depth - 2, 2)], klo, after),
@@ -269,55 +253,6 @@
             copy.wait_send()
 
 
-def heat_steps(n_sec, n_dp, heat, cond, patch_z, patch_x, slot, weights):
-    layers = (2,) + heat.shape[1:]
-    operands = (heat, cond, *weights)
-    operands = [pltpu.with_memory_space_constraint(x, pltpu.HBM) for x in operands]
-    taps = weights[0].shape[0]
-    return pl.pallas_call(
-        functools.partial(heat_kernel, n_sec, n_dp),
-        out_shape=(
-            jax.ShapeDtypeStruct(heat.shape, F32),
-            jax.ShapeDtypeStruct((3, PZ, PX, GY), F32),
-            jax.ShapeDtypeStruct((C1, taps), BF16),
-            jax.ShapeDtypeStruct((C1, C1), BF16),
-            jax.ShapeDtypeStruct((C1, C1), BF16),
-            jax.ShapeDtypeStruct((3 * C2, 9 * C1), BF16),
-            jax.ShapeDtypeStruct((3 * C1, 9 * C2), BF16),
-            jax.ShapeDtypeStruct((C2, C2), BF16),
-            jax.ShapeDtypeStruct((C2, C2), BF16),
-            jax.ShapeDtypeStruct((C1, C1), BF16),
-            jax.ShapeDtypeStruct((C1, C1), BF16),
-            jax.ShapeDtypeStruct((C1, C2), BF16),
-            jax.ShapeDtypeStruct((C2, C1), BF16),
-            jax.ShapeDtypeStruct((C1, GY), F32),
-            jax.ShapeDtypeStruct((16, GY), BF16),
-        ),
-        in_specs=[SMEM] * 3 + [HBM] * 8,
-        out_specs=(VMEM,) * 15,
-        scratch_shapes=[
-            pltpu.VMEM(weights[0].shape, BF16),
-            pltpu.VMEM(weights[2].shape, BF16),
-            pltpu.VMEM(weights[4].shape, BF16),
-            pltpu.VMEM(weights[5].shape, BF16),
-            pltpu.VMEM(heat.shape, F32),
-            pltpu.VMEM(heat.shape, F32),
-            pltpu.VMEM(layers, F32),
-            pltpu.VMEM(layers, F32),
-            pltpu.VMEM(layers, F32),
-            pltpu.VMEM(layers, F32),
-            pltpu.VMEM((heat.shape[0] + 2,) + heat.shape[1:], F32),
-            pltpu.SemaphoreType.DMA((8,)),
-            pltpu.SemaphoreType.DMA((4,)),
-            pltpu.SemaphoreType.DMA((4,)),
-        ],
-        compiler_params=pltpu.CompilerParams(
-            collective_id=0, has_side_effects=True, vmem_limit_bytes=16 * 2**20
-        ),
-        name="heat",
-    )(patch_z, patch_x, slot, *operands)
-
-
 def silu_and_slope(z):
     s = 0.5 * jnp.tanh(0.5 * z) + 0.5
     value = z * s
@@ -328,7 +263,7 @@
     return x[:, b * GY : (b + 1) * GY]
 
 
-def train_kernel(
+def train_part(
     scale,
     n_sec,
     n_hi,
@@ -423,12 +358,6 @@
             src_ref=like, dst_ref=like, send_sem=ssem, recv_sem=rsem, device_id=device, device_id_type=MESH
         )
 
-    barrier = pltpu.get_barrier_semaphore()
-    for d in range(1, across):
-        pl.semaphore_signal(barrier, inc=1, device_id=in_column(d)[1], device_id_type=MESH)
-    for d in range(1, n_lo):
-        pl.semaphore_signal(barrier, inc=1, device_id=in_line(d)[1], device_id_type=MESH)
-
     plane = PX * GY
     cells = PZ * plane
     small = cells // 4
@@ -547,7 +476,6 @@
     packet[0:half, :] = jnp.concatenate(forecast[0 : PZ // 2], axis=0).astype(BF16)
     packet[half : 2 * half, :] = jnp.concatenate(forecast[PZ // 2 : PZ], axis=0).astype(BF16)
     packet[2 * half : 2 * half + 16, :] = slot_tile[...]
-    pl.semaphore_wait(barrier, n_lo - 1 + across - 1)
     for d in range(1, n_hi):
         peer, device = in_part(d)
         send(packet, pbuf.at[d], s3, r3, device)
@@ -798,7 +726,62 @@
         copy.wait_send()
 
 
-def train(scale, n_sec, n_hi, n_lo, slot, patch, weights):
+def whole_kernel(n_sec, n_hi, n_lo, scale, *refs):
+    ins, refs = refs[:11], refs[11:]
+    (heat_out, pred_out, buf2), refs = refs[:3], refs[3:]
+    made, refs = refs[:14], refs[14:]
+    heat_scratch, train_scratch = refs[:14], refs[14:]
+    sec = lax.axis_index("section")
+    dp = lax.axis_index("dp")
+    hi = lax.div(dp, n_lo)
+    lo = lax.rem(dp, n_lo)
+    across = n_sec * n_hi
+    mine = sec * n_hi + hi
+    n_dp = n_hi * n_lo
+    total = n_sec * n_dp
+    me = sec * n_dp + dp
+    barrier = pltpu.get_barrier_semaphore()
+    at_start = jnp.logical_and(lo == 0, me > 0)
+    at_end = jnp.logical_and(lo == n_lo - 1, me < total - 1)
+    outside = jnp.logical_or(at_start, at_end)
+
+    def signal(section, index):
+        pl.semaphore_signal(barrier, inc=1, device_id=(section, index), device_id_type=MESH)
+
+    def enter():
+        @pl.when(at_start)
+        def _():
+            signal(lax.div(me - 1, n_dp), lax.rem(me - 1, n_dp))
+
+        @pl.when(at_end)
+        def _():
+            signal(lax.div(me + 1, n_dp), lax.rem(me + 1, n_dp))
+
+        for d in range(1, n_lo):
+            signal(sec, hi * n_lo + lax.rem(lo + d, n_lo))
+        for d in range(1, across):
+            peer = lax.rem(mine + d, across)
+            signal(lax.div(peer, n_hi), lax.rem(peer, n_hi) * n_lo + lo)
+
+    def ready():
+        peers = n_lo - 1 + across - 1
+
+        @pl.when(outside)
+        def _():
+            pl.semaphore_wait(barrier, peers + 1)
+
+        @pl.when(jnp.logical_not(outside))
+        def _():
+            pl.semaphore_wait(barrier, peers)
+
+    heat_part(enter, ready, n_sec, n_dp, *ins, heat_out, *made, *heat_scratch)
+    patch, *weights, slot_tile = made
+    train_part(scale, n_sec, n_hi, n_lo, slot_tile, patch, *weights, pred_out, buf2, *train_scratch)
+
+
+def whole(scale, n_sec, n_hi, n_lo, heat, cond, patch_z, patch_x, slot, weights):
+    layers = (2,) + heat.shape[1:]
+    taps = weights[0].shape[0]
     cells = PZ * PX * GY
     small = cells // 4
     per = GROWS // (n_lo * n_hi)
@@ -806,15 +789,46 @@
     n_y = n_lo // 2
     first = -(-(27 + 32) // (per * n_lo))
     dma = pltpu.SemaphoreType.DMA
+    operands = (heat, cond, *weights)
+    operands = [pltpu.with_memory_space_constraint(x, pltpu.HBM) for x in operands]
     return pl.pallas_call(
-        functools.partial(train_kernel, scale, n_sec, n_hi, n_lo),
+        functools.partial(whole_kernel, n_sec, n_hi, n_lo, scale),
         out_shape=(
+            jax.ShapeDtypeStruct(heat.shape, F32),
             jax.ShapeDtypeStruct((2, PZ * PX, GY), F32),
             jax.ShapeDtypeStruct((across, per, GY), BF16),
         ),
-        in_specs=[VMEM] * 14,
-        out_specs=(VMEM, VMEM),
+        in_specs=[SMEM] * 3 + [HBM] * 8,
+        out_specs=(VMEM,) * 3,
         scratch_shapes=[
+            pltpu.VMEM((3, PZ, PX, GY), F32),
+            pltpu.VMEM((C1, taps), BF16),
+            pltpu.VMEM((C1, C1), BF16),
+            pltpu.VMEM((C1, C1), BF16),
+            pltpu.VMEM((3 * C2, 9 * C1), BF16),
+            pltpu.VMEM((3 * C1, 9 * C2), BF16),
+            pltpu.VMEM((C2, C2), BF16),
+            pltpu.VMEM((C2, C2), BF16),
+            pltpu.VMEM((C1, C1), BF16),
+            pltpu.VMEM((C1, C1), BF16),
+            pltpu.VMEM((C1, C2), BF16),
+            pltpu.VMEM((C2, C1), BF16),
+            pltpu.VMEM((C1, GY), F32),
+            pltpu.VMEM((16, GY), BF16),
+            pltpu.VMEM(weights[0].shape, BF16),
+            pltpu.VMEM(weights[2].shape, BF16),
+            pltpu.VMEM(weights[4].shape, BF16),
+            pltpu.VMEM(weights[5].shape, BF16),
+            pltpu.VMEM(heat.shape, F32),
+            pltpu.VMEM(heat.shape, F32),
+            pltpu.VMEM(layers, F32),
+            pltpu.VMEM(layers, F32),
+            pltpu.VMEM(layers, F32),
+            pltpu.VMEM(layers, F32),
+            pltpu.VMEM((heat.shape[0] + 2,) + heat.shape[1:], F32),
+            dma((8,)),
+            dma((4,)),
+            dma((4,)),
             pltpu.VMEM((PZ * PX * C1, GY), F32),
             pltpu.VMEM((C1, cells), BF16),
             pltpu.VMEM((C1, cells), BF16),
@@ -851,10 +865,10 @@
             dma,
         ],
         compiler_params=pltpu.CompilerParams(
-            collective_id=1, has_side_effects=True, vmem_limit_bytes=32 * 2**20
+            collective_id=0, has_side_effects=True, vmem_limit_bytes=48 * 2**20
         ),
-        name="train",
-    )(slot, patch, *weights)
+        name="whole",
+    )(patch_z, patch_x, slot, *operands)
 
 
 def finish_kernel(heat_in, pred_in, grad_in, heat_out, pred_out, grad_out, done):
@@ -904,11 +918,10 @@
     n_lo = LINE
     n_hi = n_dp // n_lo
     weights = (w_stem.T, w_lift, w_down.T, w_deep, w_merge, w_out)
-    heat_two, patch, *ready, slot = heat_steps(
-        n_sec, n_dp, heat_start, conductivity, patch_z, patch_x, slot_table, weights
+    scale = 1.0 / (n_sec * n_dp * PZ * PX * GY)
+    heat_two, preds, partials = whole(
+        scale, n_sec, n_hi, n_lo, heat_start, conductivity, patch_z, patch_x, slot_table, weights
     )
-    scale = 1.0 / (n_sec * n_dp * PZ * PX * GY)
-    preds, partials = train(scale, n_sec, n_hi, n_lo, slot, patch, ready)
     return finish(heat_two, preds, partials)
 
 

time: 38.7 us -> 38.1 us (0.984)
  Pallas kernels: 36 us -> 35.4 us
    pallas_call x2 -> x1, Pallas kernels: 34.7 us -> 34.1 us  [whole(): pl.pallas_call(functools.partial(whole_kernel, n_sec, n_hi, n_lo, scale),...]
where the time goes in v6:
time: 38.1 us; the launch traced here: 38 us
  Pallas kernels  35.4 us (93%)
  between operations  2.58 us (7%)
    pallas_call x1, Pallas kernels, whole(): pl.pallas_call(functools.partial(whole_kernel, n_sec, n_hi, n_lo, scale),...  34.1 us
    pallas_call x1, Pallas kernels, finish(): pl.pallas_call(finish_kernel, out_shape=(jax.ShapeDtypeStruct(heat.shape,...  1.32 us

profile of v6, /device:TPU:1, one launch (start us, length us, event | category | flops | bytes accessed | tf_op | source)
XLA Modules:
  0.0 38.0 jit_solution(12229533927950900782)
XLA Ops:
  2.6 34.1 %whole.1 = (f32[16,32,128]{2,1,0:T(8,128)S(1)}, f32[2,32,128]{2,1,0:T(8,128)S(1)}, bf16[32,16,128]{2,1,0:T(8,128)(2,1)S(1)}) custom-call(s32[1]{0:T(128)S(6)} %copy.14.refs_0_, s32[1]{0:T(128)S(6)} %copy.15.refs_1_, s32[1]{0:T(128)S(6)} %copy.16.refs_2_, f32[16,32,128]{2,1,0:T(8,128)} %refs_3_.1, f32[16,32,128]{2,1,0:T(8,128)} %refs_4_.1, ...), custom_call_target="tpu_custom_call" | custom-call | tf_op jit(solution)/shard_map/whole/pallas_call | solution.py:794
  36.7 1.3 %finish.1 = (f32[16,32,128]{2,1,0:T(8,128)}, bf16[2,4,8,128]{3,2,1,0:T(8,128)(2,1)}, f32[16,128]{1,0:T(8,128)}) custom-call(f32[16,32,128]{2,1,0:T(8,128)S(1)} %get-tuple-element.6.heat_in, f32[2,32,128]{2,1,0:T(8,128)S(1)} %get-tuple-element.7.pred_in, bf16[32,16,128]{2,1,0:T(8,128)(2,1)S(1)} %get-tuple-element.8.grad_in), custom_call_target="tpu_custom_call" | custom-call | tf_op jit(solution)/shard_map/finish/pallas_call | solution.py:888

commit v7 on v6

--- a/solution.py
+++ b/solution.py
@@ -298,20 +298,13 @@
     pair,
     grads,
     packet,
-    cbuf,
-    half_ref,
     buf1,
-    buf_late,
     acc,
     pbuf,
     q_ref,
     qbuf,
     s1,
     r1,
-    sc,
-    rc,
-    s5,
-    r5,
     s2,
     r2,
     s3,
@@ -325,18 +318,10 @@
     lo = lax.rem(dp, n_lo)
     across = n_sec * n_hi
     mine = sec * n_hi + hi
-    n_y = n_lo // 2
-    core = lax.rem(lo, 2)
-    other = 1 - core
-    y = lax.div(lo, 2)
 
     def in_line(d):
         peer = lax.rem(lo + d, n_lo)
         return peer, (sec, hi * n_lo + peer)
-
-    def in_y(d):
-        peer = lax.rem(y + d, n_y)
-        return peer, (sec, hi * n_lo + 2 * peer + core)
 
     def in_column(d):
         peer = lax.rem(mine + d, across)
@@ -522,7 +507,7 @@
             low, piece(2 * j, True), piece(2 * j + 1, False)
         )
 
-    per = grads.shape[3]
+    per = grads.shape[2]
     first = -(-(27 + 32) // (per * n_lo))
     top = n_hi - (27 + 32 + 27 * C1) // (per * n_lo)
     tail = first + top
@@ -530,38 +515,19 @@
     def emit(hi_):
         for lo_ in range(n_lo):
             start = (hi_ * n_lo + lo_) * per
-            grads[lo_ % 2, lo_ // 2, (hi_ + top) % n_hi] = pack[start : start + per, :].astype(BF16)
+            grads[lo_, (hi_ + top) % n_hi] = pack[start : start + per, :].astype(BF16)
 
     for h in range(first, n_hi - top):
         emit(h)
 
-    def swap(begin, count, i):
-        return send(
-            grads.at[other, :, pl.ds(begin, count)],
-            cbuf.at[:, pl.ds(begin, count)],
-            sc.at[i],
-            rc.at[i],
-            (sec, hi * n_lo + 2 * y + other),
-        )
-
-    def chip_sum(begin, count, copy, i):
-        copy.wait_recv()
-        part = slice(begin, begin + count)
-        for y_ in range(n_y):
-            total = grads[core, y_, part].astype(F32) + cbuf[y_, part].astype(F32)
-            half_ref[y_, part] = total.astype(BF16)
-        for d in range(1, n_y):
-            peer, device = in_y(d)
-            send(
-                half_ref.at[peer, pl.ds(begin, count)],
-                buf1.at[d - 1, pl.ds(begin, count)],
-                s1.at[i],
-                r1.at[i],
-                device,
-            )
-        return group(buf1.at[:, pl.ds(begin, count)], s1.at[i], r1.at[i], device)
-
-    swap_down = swap(tail, n_hi - tail, 0)
+    def scatter(begin, count, i):
+        part = pl.ds(begin, count)
+        for d in range(1, n_lo):
+            peer, device = in_line(d)
+            send(grads.at[peer, part], buf1.at[d - 1, part], s1.at[i], r1.at[i], device)
+        return group(buf1.at[:, part], s1.at[i], r1.at[i], device)
+
+    early = scatter(tail, n_hi - tail, 0)
 
     def twice(x):
         pair[:, 0:C1] = x
@@ -593,10 +559,6 @@
     pack[base + 1 : GROWS, :] = jnp.zeros((GROWS - base - 1, GY), F32)
 
 
-    for h in range(n_hi - top, n_hi):
-        emit(h)
-    swap_join = swap(0, top, 1)
-
     blank = jnp.zeros((C2, GY), BF16)
     for dz in range(3):
         for dx in range(3):
@@ -609,7 +571,6 @@
                     colsz[j * C2 : (j + 1) * C2, b * GY : (b + 1) * GY] = (
                         block(dz_down, sz * hx + sx) if inside else blank
                     )
-    early_down = chip_sum(tail, n_hi - tail, swap_down, 0)
     d_shifted = mm(wback[...], colsz[...])
     d_pooled = []
     for b in range(hz * hx):
@@ -619,7 +580,6 @@
         total = total + jnp.where(lane64 == 0, 0.0, pltpu.roll(whole[2 * C1 : 3 * C1], 1, 1))
         d_pooled.append(rounded(total) * 0.25)
 
-    early_join = chip_sum(0, top, swap_join, 1)
     lift_t = w_lift_t[...]
     d_stem = jnp.zeros((C1, C1), F32)
     for z in range(PZ):
@@ -655,33 +615,23 @@
     pack[27 : 27 + 32, :] = jnp.where(low32, pair[pl.ds(0, 32, stride=2), :], pair[pl.ds(1, 32, stride=2), :])
 
 
-    for h in range(first):
+    for h in list(range(first)) + list(range(n_hi - top, n_hi)):
         emit(h)
-    for d in range(1, n_lo):
-        peer, device = in_line(d)
-        send(
-            grads.at[lax.rem(peer, 2), lax.div(peer, 2), pl.ds(top, first)],
-            buf_late.at[d - 1],
-            s5,
-            r5,
-            device,
-        )
-    late = group(buf_late, s5, r5, device)
-
-    for copy in (early_down, early_join):
-        copy.wait_recv()
-    for h in range(first, n_hi):
+    late = scatter(0, tail, 1)
+
+    def line_sum(h):
         at = (h + top) % n_hi
-        value = half_ref[y, at].astype(F32)
-        for d in range(n_y - 1):
+        value = grads[lo, at].astype(F32)
+        for d in range(n_lo - 1):
             value = value + buf1[d, at].astype(F32)
         acc[h] = value.astype(BF16)
+
+    early.wait_recv()
+    for h in range(first, n_hi - top):
+        line_sum(h)
     late.wait_recv()
-    for h in range(first):
-        value = grads[core, y, h + top].astype(F32)
-        for d in range(n_lo - 1):
-            value = value + buf_late[d, h].astype(F32)
-        acc[h] = value.astype(BF16)
+    for h in list(range(first)) + list(range(n_hi - top, n_hi)):
+        line_sum(h)
     ring = 8
     far_first = sorted(range(1, n_hi + 1), key=lambda e: (e == n_hi, -min(e % ring, ring - e % ring)))
     for e in far_first:
@@ -722,7 +672,7 @@
         pred_out[s] = value
 
     partials.wait_recv()
-    for copy in (swap_down, swap_join, packets, early_down, early_join, late, routed, partials):
+    for copy in (packets, early, late, routed, partials):
         copy.wait_send()
 
 
@@ -757,11 +707,11 @@
         def _():
             signal(lax.div(me + 1, n_dp), lax.rem(me + 1, n_dp))
 
+        for d in sorted(range(1, across), key=lambda d: (d % 8 == 0, d % 8)):
+            peer = lax.rem(mine + d, across)
+            signal(lax.div(peer, n_hi), lax.rem(peer, n_hi) * n_lo + lo)
         for d in range(1, n_lo):
             signal(sec, hi * n_lo + lax.rem(lo + d, n_lo))
-        for d in range(1, across):
-            peer = lax.rem(mine + d, across)
-            signal(lax.div(peer, n_hi), lax.rem(peer, n_hi) * n_lo + lo)
 
     def ready():
         peers = n_lo - 1 + across - 1
@@ -786,8 +736,6 @@
     small = cells // 4
     per = GROWS // (n_lo * n_hi)
     across = n_sec * n_hi
-    n_y = n_lo // 2
-    first = -(-(27 + 32) // (per * n_lo))
     dma = pltpu.SemaphoreType.DMA
     operands = (heat, cond, *weights)
     operands = [pltpu.with_memory_space_constraint(x, pltpu.HBM) for x in operands]
@@ -841,22 +789,15 @@
             pltpu.VMEM((9 * C2, small), BF16),
             pltpu.VMEM((GROWS, GY), F32),
             pltpu.VMEM((C1, GY), F32),
-            pltpu.VMEM((2, n_y, n_hi, per, GY), BF16),
+            pltpu.VMEM((n_lo, n_hi, per, GY), BF16),
             pltpu.VMEM((PZ * PX + 16, GY), BF16),
-            pltpu.VMEM((n_y, n_hi, per, GY), BF16),
-            pltpu.VMEM((n_y, n_hi, per, GY), BF16),
-            pltpu.VMEM((n_y - 1, n_hi, per, GY), BF16),
-            pltpu.VMEM((n_lo - 1, first, per, GY), BF16),
+            pltpu.VMEM((n_lo - 1, n_hi, per, GY), BF16),
             pltpu.VMEM((n_hi, per, GY), BF16),
             pltpu.VMEM((n_hi, PZ * PX + 16, GY), BF16),
             pltpu.VMEM((2 * n_lo, PZ * PX, GY), BF16),
             pltpu.VMEM((n_lo - 1, 2, PZ * PX, GY), BF16),
             dma((2,)),
             dma((2,)),
-            dma((2,)),
-            dma((2,)),
-            dma,
-            dma,
             dma,
             dma,
             dma,

time: 38.1 us -> 38.3 us (level)
  no operation moved by 1% of the time
where the time goes in v7:
time: 38.3 us; the launch traced here: 38.2 us
  Pallas kernels  35.7 us (93%)
  between operations  2.58 us (7%)
    pallas_call x1, Pallas kernels, whole(): pl.pallas_call(functools.partial(whole_kernel, n_sec, n_hi, n_lo, scale),...  34.3 us
    pallas_call x1, Pallas kernels, finish(): pl.pallas_call(finish_kernel, out_shape=(jax.ShapeDtypeStruct(heat.shape,...  1.32 us

profile of v7, /device:TPU:1, one launch (start us, length us, event | category | flops | bytes accessed | tf_op | source)
XLA Modules:
  0.0 38.2 jit_solution(3196763347200790978)
XLA Ops:
  2.6 34.3 %whole.1 = (f32[16,32,128]{2,1,0:T(8,128)S(1)}, f32[2,32,128]{2,1,0:T(8,128)S(1)}, bf16[32,16,128]{2,1,0:T(8,128)(2,1)S(1)}) custom-call(s32[1]{0:T(128)S(6)} %copy.14.refs_0_, s32[1]{0:T(128)S(6)} %copy.15.refs_1_, s32[1]{0:T(128)S(6)} %copy.16.refs_2_, f32[16,32,128]{2,1,0:T(8,128)} %refs_3_.1, f32[16,32,128]{2,1,0:T(8,128)} %refs_4_.1, ...), custom_call_target="tpu_custom_call" | custom-call | tf_op jit(solution)/shard_map/whole/pallas_call | solution.py:742
  36.9 1.3 %finish.1 = (f32[16,32,128]{2,1,0:T(8,128)}, bf16[2,4,8,128]{3,2,1,0:T(8,128)(2,1)}, f32[16,128]{1,0:T(8,128)}) custom-call(f32[16,32,128]{2,1,0:T(8,128)S(1)} %get-tuple-element.6.heat_in, f32[2,32,128]{2,1,0:T(8,128)S(1)} %get-tuple-element.7.pred_in, bf16[32,16,128]{2,1,0:T(8,128)(2,1)S(1)} %get-tuple-element.8.grad_in), custom_call_target="tpu_custom_call" | custom-call | tf_op jit(solution)/shard_map/finish/pallas_call | solution.py:829

commit v8 on v7

--- a/solution.py
+++ b/solution.py
@@ -38,6 +38,7 @@
 def heat_part(
     enter,
     ready,
+    meanwhile,
     n_sec,
     n_dp,
     pz_ref,
@@ -212,6 +213,12 @@
     column = jnp.sum(jnp.where(eye, jnp.broadcast_to(row64, (C1, C1)), 0.0), axis=1, keepdims=True)
     proj_col[...] = jnp.broadcast_to(column, proj_col.shape)
 
+    pz = pz_ref[0]
+    px = px_ref[0]
+    for z in range(PZ):
+        patch_ref[1, z] = k_ref[pz + z, pl.ds(px, PX), :]
+    meanwhile()
+
     @pl.when(below)
     def _():
         for copy in upward:
@@ -235,11 +242,8 @@
     out_ref[end] = step(h1[end], h1[depth], h1[depth + 1], k_ref[end - 1], k_ref[end], kh[0])
     second(1)
     second(end - 1)
-    pz = pz_ref[0]
-    px = px_ref[0]
     for z in range(PZ):
         patch_ref[0, z] = h1[1 + pz + z, pl.ds(px, PX), :]
-        patch_ref[1, z] = k_ref[pz + z, pl.ds(px, PX), :]
         patch_ref[2, z] = out_ref[pz + z, pl.ds(px, PX), :]
 
     @pl.when(above)
@@ -261,6 +265,30 @@
 
 def block(x, b):
     return x[:, b * GY : (b + 1) * GY]
+
+
+def stem_columns(patch_ref, tall, channel):
+    row8 = lax.broadcasted_iota(jnp.int32, (PX, GY), 0)
+    lane8 = lax.broadcasted_iota(jnp.int32, (PX, GY), 1)
+    for dx in range(3):
+        for dy in range(3):
+            shifted = []
+            for z in range(PZ):
+                v = rounded(patch_ref[channel, z])
+                if dx == 0:
+                    v = jnp.where(row8 == 0, 0.0, pltpu.roll(v, 1, 0))
+                elif dx == 2:
+                    v = jnp.where(row8 == PX - 1, 0.0, pltpu.roll(v, PX - 1, 0))
+                if dy == 0:
+                    v = jnp.where(lane8 == 0, 0.0, pltpu.roll(v, 1, 1))
+                elif dy == 2:
+                    v = jnp.where(lane8 == GY - 1, 0.0, pltpu.roll(v, GY - 1, 1))
+                shifted.append(v)
+            for dz in range(3):
+                r = ((dz * 3 + dx) * 3 + dy) * 2 + channel
+                for z in range(PZ):
+                    if 0 <= z + dz - 1 < PZ:
+                        tall[pl.ds(z * PX * C1 + r, PX, stride=C1), :] = shifted[z + dz - 1]
 
 
 def train_part(
@@ -350,27 +378,7 @@
     lane8 = lax.broadcasted_iota(jnp.int32, (PX, GY), 1)
     lane64 = lax.broadcasted_iota(jnp.int32, (C1, GY), 1)
 
-    tall[...] = jnp.zeros_like(tall)
-    for channel in range(2):
-        for dx in range(3):
-            for dy in range(3):
-                shifted = []
-                for z in range(PZ):
-                    v = rounded(patch_ref[channel, z])
-                    if dx == 0:
-                        v = jnp.where(row8 == 0, 0.0, pltpu.roll(v, 1, 0))
-                    elif dx == 2:
-                        v = jnp.where(row8 == PX - 1, 0.0, pltpu.roll(v, PX - 1, 0))
-                    if dy == 0:
-                        v = jnp.where(lane8 == 0, 0.0, pltpu.roll(v, 1, 1))
-                    elif dy == 2:
-                        v = jnp.where(lane8 == GY - 1, 0.0, pltpu.roll(v, GY - 1, 1))
-                    shifted.append(v)
-                for dz in range(3):
-                    r = ((dz * 3 + dx) * 3 + dy) * 2 + channel
-                    for z in range(PZ):
-                        if 0 <= z + dz - 1 < PZ:
-                            tall[pl.ds(z * PX * C1 + r, PX, stride=C1), :] = shifted[z + dz - 1]
+    stem_columns(patch_ref, tall, 0)
     for b in range(PZ * PX):
         cols[:, b * GY : (b + 1) * GY] = tall[b * C1 : (b + 1) * C1, :].astype(BF16)
 
@@ -396,7 +404,6 @@
             pooled.append(rounded((block(both, 2 * xx) + block(both, 2 * xx + 1)) * 0.25))
 
     hz, hx = PZ // 2, PX // 2
-    nothing = jnp.zeros((C1, GY), BF16)
     pooled = [v.astype(BF16) for v in pooled]
     for dz in range(3):
         for dx in range(3):
@@ -406,9 +413,9 @@
                     sz, sx = z + dz - 1, x + dx - 1
                     inside = 0 <= sz < hz and 0 <= sx < hx
                     b = z * hx + x
-                    colsd[r : r + C1, b * GY : (b + 1) * GY] = pooled[sz * hx + sx] if inside else nothing
+                    if inside:
+                        colsd[r : r + C1, b * GY : (b + 1) * GY] = pooled[sz * hx + sx]
     depth = 9 * C1
-    colsd[depth : depth + C1, :] = jnp.zeros((C1, small), BF16)
     products = mm(w_down[...], colsd[0:depth, :])
     lane128 = lax.broadcasted_iota(jnp.int32, (C2, GY), 1)
 
@@ -559,7 +566,6 @@
     pack[base + 1 : GROWS, :] = jnp.zeros((GROWS - base - 1, GY), F32)
 
 
-    blank = jnp.zeros((C2, GY), BF16)
     for dz in range(3):
         for dx in range(3):
             j = dz * 3 + dx
@@ -568,9 +574,10 @@
                     sz, sx = z - (dz - 1), x - (dx - 1)
                     inside = 0 <= sz < hz and 0 <= sx < hx
                     b = z * hx + x
-                    colsz[j * C2 : (j + 1) * C2, b * GY : (b + 1) * GY] = (
-                        block(dz_down, sz * hx + sx) if inside else blank
-                    )
+                    if inside:
+                        colsz[j * C2 : (j + 1) * C2, b * GY : (b + 1) * GY] = block(
+                            dz_down, sz * hx + sx
+                        )
     d_shifted = mm(wback[...], colsz[...])
     d_pooled = []
     for b in range(hz * hx):
@@ -724,8 +731,15 @@
         def _():
             pl.semaphore_wait(barrier, peers)
 
-    heat_part(enter, ready, n_sec, n_dp, *ins, heat_out, *made, *heat_scratch)
     patch, *weights, slot_tile = made
+    tall, colsd, colsz = train_scratch[0], train_scratch[8], train_scratch[9]
+
+    def meanwhile():
+        for cleared in (tall, colsd, colsz):
+            cleared[...] = jnp.zeros_like(cleared)
+        stem_columns(patch, tall, 1)
+
+    heat_part(enter, ready, meanwhile, n_sec, n_dp, *ins, heat_out, *made, *heat_scratch)
     train_part(scale, n_sec, n_hi, n_lo, slot_tile, patch, *weights, pred_out, buf2, *train_scratch)
 
 

time: 38.3 us -> 38 us (level)
  Pallas kernels: 35.7 us -> 35.3 us
where the time goes in v8:
time: 38 us; the launch traced here: 37.9 us
  Pallas kernels  35.3 us (93%)
  between operations  2.58 us (7%)
    pallas_call x1, Pallas kernels, whole(): pl.pallas_call(functools.partial(whole_kernel, n_sec, n_hi, n_lo, scale),...  34 us
    pallas_call x1, Pallas kernels, finish(): pl.pallas_call(finish_kernel, out_shape=(jax.ShapeDtypeStruct(heat.shape,...  1.32 us

profile of v8, /device:TPU:1, one launch (start us, length us, event | category | flops | bytes accessed | tf_op | source)
XLA Modules:
  0.0 37.9 jit_solution(5106328280689167732)
XLA Ops:
  2.6 34.0 %whole.1 = (f32[16,32,128]{2,1,0:T(8,128)S(1)}, f32[2,32,128]{2,1,0:T(8,128)S(1)}, bf16[32,16,128]{2,1,0:T(8,128)(2,1)S(1)}) custom-call(s32[1]{0:T(128)S(6)} %copy.14.refs_0_, s32[1]{0:T(128)S(6)} %copy.15.refs_1_, s32[1]{0:T(128)S(6)} %copy.16.refs_2_, f32[16,32,128]{2,1,0:T(8,128)} %refs_3_.1, f32[16,32,128]{2,1,0:T(8,128)} %refs_4_.1, ...), custom_call_target="tpu_custom_call" | custom-call | tf_op jit(solution)/shard_map/whole/pallas_call | solution.py:756
  36.6 1.3 %finish.1 = (f32[16,32,128]{2,1,0:T(8,128)}, bf16[2,4,8,128]{3,2,1,0:T(8,128)(2,1)}, f32[16,128]{1,0:T(8,128)}) custom-call(f32[16,32,128]{2,1,0:T(8,128)S(1)} %get-tuple-element.6.heat_in, f32[2,32,128]{2,1,0:T(8,128)S(1)} %get-tuple-element.7.pred_in, bf16[32,16,128]{2,1,0:T(8,128)(2,1)S(1)} %get-tuple-element.8.grad_in), custom_call_target="tpu_custom_call" | custom-call | tf_op jit(solution)/shard_map/finish/pallas_call | solution.py:843

commit v9 on v8

--- a/solution.py
+++ b/solution.py
@@ -468,12 +468,6 @@
     packet[0:half, :] = jnp.concatenate(forecast[0 : PZ // 2], axis=0).astype(BF16)
     packet[half : 2 * half, :] = jnp.concatenate(forecast[PZ // 2 : PZ], axis=0).astype(BF16)
     packet[2 * half : 2 * half + 16, :] = slot_tile[...]
-    for d in range(1, n_hi):
-        peer, device = in_part(d)
-        send(packet, pbuf.at[d], s3, r3, device)
-    packets = group(pbuf.at[pl.ds(1, n_hi - 1)], s3, r3, device)
-    pbuf[0] = packet[...]
-
     d_lifted = jnp.concatenate(gathered, axis=1).astype(BF16)
     d_deeper = mm(w_coarse_t[...], d_lifted)
     dz_deep = (rounded(d_deeper) * slope_deep).astype(BF16)
@@ -535,6 +529,11 @@
         return group(buf1.at[:, part], s1.at[i], r1.at[i], device)
 
     early = scatter(tail, n_hi - tail, 0)
+    for d in range(1, n_hi):
+        peer, device = in_part(d)
+        send(packet, pbuf.at[d], s3, r3, device)
+    packets = group(pbuf.at[pl.ds(1, n_hi - 1)], s3, r3, device)
+    pbuf[0] = packet[...]
 
     def twice(x):
         pair[:, 0:C1] = x

time: 38 us -> 38.2 us (level)
  no operation moved by 1% of the time
where the time goes in v9:
time: 38.2 us; the launch traced here: 38.1 us
  Pallas kernels  35.5 us (93%)
  between operations  2.58 us (7%)
    pallas_call x1, Pallas kernels, whole(): pl.pallas_call(functools.partial(whole_kernel, n_sec, n_hi, n_lo, scale),...  34.2 us
    pallas_call x1, Pallas kernels, finish(): pl.pallas_call(finish_kernel, out_shape=(jax.ShapeDtypeStruct(heat.shape,...  1.32 us

profile of v9, /device:TPU:1, one launch (start us, length us, event | category | flops | bytes accessed | tf_op | source)
XLA Modules:
  0.0 38.1 jit_solution(16312020320667911169)
XLA Ops:
  2.6 34.2 %whole.1 = (f32[16,32,128]{2,1,0:T(8,128)S(1)}, f32[2,32,128]{2,1,0:T(8,128)S(1)}, bf16[32,16,128]{2,1,0:T(8,128)(2,1)S(1)}) custom-call(s32[1]{0:T(128)S(6)} %copy.14.refs_0_, s32[1]{0:T(128)S(6)} %copy.15.refs_1_, s32[1]{0:T(128)S(6)} %copy.16.refs_2_, f32[16,32,128]{2,1,0:T(8,128)} %refs_3_.1, f32[16,32,128]{2,1,0:T(8,128)} %refs_4_.1, ...), custom_call_target="tpu_custom_call" | custom-call | tf_op jit(solution)/shard_map/whole/pallas_call | solution.py:755
  36.8 1.3 %finish.1 = (f32[16,32,128]{2,1,0:T(8,128)}, bf16[2,4,8,128]{3,2,1,0:T(8,128)(2,1)}, f32[16,128]{1,0:T(8,128)}) custom-call(f32[16,32,128]{2,1,0:T(8,128)S(1)} %get-tuple-element.6.heat_in, f32[2,32,128]{2,1,0:T(8,128)S(1)} %get-tuple-element.7.pred_in, bf16[32,16,128]{2,1,0:T(8,128)(2,1)S(1)} %get-tuple-element.8.grad_in), custom_call_target="tpu_custom_call" | custom-call | tf_op jit(solution)/shard_map/finish/pallas_call | solution.py:842
